TPU v7x, 256 devices: a whole 4x4x8 slice. The times are simulated.
256 devices in a mesh: px: 32 (over z, y), py: 8 (over x, core).
Axes of the slice: x: 4, y: 4, z: 8, core: 2. Of those that a mesh axis runs over, the one named last changes fastest.
Arguments:
- dofs: float32 [9, 20, 65536], P(None, None, ('px', 'py')), may hold values from -6 to 6
- star: float32 [3, 9, 9, 65536], P(None, None, None, ('px', 'py')), may hold values from -2 to 2
- flux_local: float32 [4, 9, 9, 65536], P(None, None, None, ('px', 'py')), may hold values from -0.5 to 0.5
- flux_neigh: float32 [4, 9, 9, 65536], P(None, None, None, ('px', 'py')), may hold values from -0.5 to 0.5
- time_stiff: float32 [3, 20, 20], replicated, may hold values from -1.25 to 1.25
- volume_stiff: float32 [3, 20, 20], replicated, may hold values from -0.15625 to 0.15625
- face_project: float32 [4, 10, 20], replicated, may hold values from -1.25 to 1.25
- face_rotate: float32 [3, 10, 10], replicated, may hold values from -2 to 2
- face_lift: float32 [4, 20, 10], replicated, may hold values from -2 to 2
- cluster: int32 [65536], P(('px', 'py')), may hold values from 0 to 1, as said below
- neighbors: int32 [4, 65536], P(None, ('px', 'py')), may hold values from -1 to 65535, as said below
- face_kind: int32 [4, 65536], P(None, ('px', 'py')), may hold values from 0 to 11
Outputs:
- solution: float32 [9, 20, 65536], P(None, None, ('px', 'py'))
Inputs may be any that keep to these rules, and one draw needn't show every extreme that they name: 0 marks the fine cluster, 1 the coarse cluster. `neighbors`: devices are numbered px index times the devices along py plus py index, and element l of device r has global index r * 256 + l. -1 marks a face on the outer boundary. Every face has an element of the same device across it, except that an element with local index k * 32 + m (k < 4, m < 32) has at most one face whose neighbour lies on the device one step lower along px (k = 0), higher along px (k = 1), lower along py (k = 2) or higher along py (k = 3), at a local index from (k xor 1) * 32 to (k xor 1) * 32 + 31; where that device does not exist the face is -1.
All inputs are finite; a program needn't handle non-finite values.
Results may differ from a plain program's by a relative error of at most 0.0003.
Values sent between devices are 32-bit elements; how exact they have to be, the bound alone decides.
No kernel may reach another device: no remote copies, remote signals or barrier semaphores. Data moves between devices by JAX's collectives and lax.ppermute only.
A program may use at most 128 MiB of HBM per device.

v0:
```python
import math
from functools import partial

import jax
import jax.numpy as jnp
from jax import lax
from jax.experimental import pallas as pl
from jax.experimental.pallas import tpu as pltpu
from jax.sharding import PartitionSpec as P

ORDER = 4
NS = 32
Q = 9
B = 24
FB = 16
LANES = 128
STATIC = 42
F32 = jnp.float32
BF16 = jnp.bfloat16
HIGHEST = lax.Precision.HIGHEST
STEP = 0.4


def series(start, stop):
    return [
        (stop ** (power + 1) - start ** (power + 1)) / math.factorial(power + 1)
        for power in range(ORDER)
    ]


FIRST = series(0.0, STEP)
SECOND = series(STEP, 2.0 * STEP)


def halves(x):
    high = x.astype(BF16)
    return high, (x - high.astype(F32)).astype(BF16)


def stacked(x):
    high = x.astype(BF16).astype(F32)
    rest = jnp.zeros((8, x.shape[1]), F32)
    return jnp.concatenate([high, x - high, high, rest], axis=0).astype(BF16)


def mm(a, b):
    return jnp.dot(a, b, preferred_element_type=F32)


def group(lg):
    return pl.ds(lg * LANES, LANES)


def transpose_quarters(four):
    quarter = lax.broadcasted_iota(jnp.int32, (8, LANES), 1) // NS
    out = []
    for k in range(4):
        total = None
        for m in range(4):
            shift = (NS * (m - k)) % LANES
            moved = pltpu.roll(four[m], shift, 1) if shift else four[m]
            total = moved if total is None else jnp.where(quarter == m, moved, total)
        out.append(total)
    return out


def spread(mat, width):
    rows = lax.broadcasted_iota(jnp.int32, (20, width), 0)
    cols = lax.broadcasted_iota(jnp.int32, (20, width), 1)
    both = ((cols == rows) | (cols == rows + B)).astype(F32)
    last = (cols == rows + 2 * B).astype(F32)
    high = mat.astype(BF16).astype(F32)
    low = (mat - high).astype(BF16).astype(F32)
    return mm(high.astype(BF16), both.astype(BF16)) + mm(low.astype(BF16), last.astype(BF16))


def prepare(time_ref, volume_ref, project_ref, rotate_ref, lift_ref, wt_ref, wb_ref, wl_ref, tmp_ref, big_ref):
    width = wt_ref.shape[1]
    tmp_ref[...] = jnp.zeros_like(tmp_ref)
    for d in range(3):
        tmp_ref[B * d : B * d + 20, :] = spread(-time_ref[d], width)
    wt_ref[...] = tmp_ref[: wt_ref.shape[0], :].astype(BF16)
    tmp_ref[...] = jnp.zeros_like(tmp_ref)
    for d in range(3):
        tmp_ref[B * d : B * d + 20, :] = spread(volume_ref[d], width)
    for j in range(4):
        at = 3 * B + FB * j
        tmp_ref[at : at + 10, :] = spread(project_ref[j], width)
    wb_ref[...] = tmp_ref[...].astype(BF16)
    rows = lax.broadcasted_iota(jnp.int32, (10, 256), 0)
    cols = lax.broadcasted_iota(jnp.int32, (10, 256), 1)
    total = jnp.zeros((20, 256), F32)
    for i in range(4):
        for t in range(3):
            part = jnp.dot(lift_ref[i], rotate_ref[t], precision=HIGHEST, preferred_element_type=F32)
            place = (cols == rows + (3 * i + t) * FB).astype(F32)
            total = total + jnp.dot(part, place, precision=HIGHEST, preferred_element_type=F32)
        place = (cols == rows + 192 + i * FB).astype(F32)
        total = total + jnp.dot(lift_ref[i], place, precision=HIGHEST, preferred_element_type=F32)
    high = total.astype(BF16).astype(F32)
    big_ref[...] = jnp.zeros_like(big_ref)
    big_ref[0:20, :] = high
    big_ref[32:52, :] = total - high
    wl_ref[...] = big_ref[...].astype(BF16)


def describe(nbr_ref, kind_ref, cluster_ref, star_ref, fluxn_ref, stat_ref):
    lanes = pl.ds(0, LANES)
    here = nbr_ref[0:1, LANES : 2 * LANES] >> 8
    remote = []
    for i in range(4):
        nbr = nbr_ref[i : i + 1, lanes]
        remote.append((nbr >= 0) & ((nbr >> 8) != here))
    spot = jnp.full((1, LANES), -1, jnp.int32)
    side = jnp.full((1, LANES), -1, jnp.int32)
    turn = jnp.full((1, LANES), -1, jnp.int32)
    face = jnp.full((1, LANES), -1, jnp.int32)
    for i in range(4):
        kind = kind_ref[i : i + 1, lanes]
        spot = jnp.where(remote[i], nbr_ref[i : i + 1, lanes] & (NS - 1), spot)
        side_i = (kind >= 3).astype(jnp.int32) + (kind >= 6).astype(jnp.int32) + (kind >= 9).astype(jnp.int32)
        side = jnp.where(remote[i], side_i, side)
        turn = jnp.where(remote[i], kind - 3 * side_i, turn)
        face = jnp.where(remote[i], i, face)
    weight = [jnp.where(r, 1.0, 0.0).astype(F32) for r in remote]
    stat_ref[27 + 3] = jnp.zeros((8, LANES), F32)
    for d in range(3):
        for p in range(Q):
            at = d * Q + p
            stat_ref[at] = star_ref[d, p, 0:8, lanes]
            stat_ref[27 + at // 8, at % 8 : at % 8 + 1] = star_ref[d, p, 8:9, lanes]
    stat_ref[41] = jnp.zeros((8, LANES), F32)
    for p in range(Q):
        total, last = None, None
        for i in range(4):
            term = fluxn_ref[i, p, 0:8, lanes] * weight[i]
            term_last = fluxn_ref[i, p, 8:9, lanes] * weight[i]
            total = term if total is None else total + term
            last = term_last if last is None else last + term_last
        stat_ref[31 + p] = total
        stat_ref[40 + p // 8, p % 8 : p % 8 + 1] = last
    fine = (cluster_ref[0:1, lanes] == 0).astype(F32)
    for row, value in enumerate((spot.astype(F32), side.astype(F32), turn.astype(F32), face.astype(F32), fine)):
        stat_ref[41, row + 1 : row + 2] = value


def stat_star(stat_ref):
    def at(d, p, q):
        n = d * Q + p
        return stat_ref[n, q : q + 1] if q < 8 else stat_ref[27 + n // 8, n % 8 : n % 8 + 1]

    return at


def stat_flux(stat_ref, p, q):
    return stat_ref[31 + p, q : q + 1] if q < 8 else stat_ref[40 + p // 8, p % 8 : p % 8 + 1]


def own_star(star_ref, lg):
    return lambda d, p, q: star_ref[d, p, q : q + 1, group(lg)]


def apply_star(star, moved_ref, lg):
    acc = [None] * Q
    for q in range(Q):
        for d in range(3):
            field = moved_ref[q, B * d : B * d + B, group(lg)]
            for p in range(Q):
                term = star(d, p, q) * field
                acc[p] = term if acc[p] is None else acc[p] + term
    return acc


def predict(dofs_ref, stars, wt_ref, term_ref, moved_ref, outs):
    width = LANES * len(stars)
    for power in range(ORDER - 1):
        source = term_ref if power else dofs_ref
        for q in range(Q):
            moved_ref[q, 0 : 3 * B, 0:width] = mm(wt_ref[...], stacked(source[q, :, 0:width]))[0 : 3 * B]
        for lg, star in enumerate(stars):
            acc = apply_star(star, moved_ref, lg)
            for p in range(Q):
                if power < ORDER - 2:
                    term_ref[p, :, group(lg)] = acc[p]
                for out_ref, coeffs in outs:
                    before = out_ref[p, :, group(lg)] if power else coeffs[0] * dofs_ref[p, :, group(lg)]
                    out_ref[p, :, group(lg)] = before + coeffs[power + 1] * acc[p]


def build_onehot(nbr_ref, kind_ref, hot_ref, tm_ref, groups):
    index = lax.broadcasted_iota(jnp.int32, (256, LANES), 0)
    here = nbr_ref[0:1, LANES : 2 * LANES] >> 8
    for lg in groups:
        for i in range(4):
            nbr = nbr_ref[i : i + 1, group(lg)]
            kind = kind_ref[i : i + 1, group(lg)]
            local = (nbr >= 0) & ((nbr >> 8) == here)
            side = (kind >= 3).astype(jnp.int32) + (kind >= 6).astype(jnp.int32) + (kind >= 9).astype(jnp.int32)
            turn = kind - 3 * side
            for j in range(4):
                pick = jnp.where(local & (side == j), nbr & 255, -1)
                hot = jnp.where(index == pick, 1.0, 0.0).astype(BF16)
                hot_ref[j * 256 : (j + 1) * 256, group(lg * 4 + i)] = hot
            for t in range(3):
                mask = jnp.where(turn == t, 1.0, 0.0).astype(F32)
                tm_ref[lg, i * 3 + t] = jnp.broadcast_to(mask, (FB, LANES)).astype(BF16)


def spread_and_project(cur_ref, wb_ref, moved_ref, face_ref, table_ref):
    for q in range(Q):
        got = mm(wb_ref[...], stacked(cur_ref[q, :, 0:256]))
        moved_ref[q, :, 0:256] = got[0 : 3 * B]
        for j in range(4):
            part = got[3 * B + FB * j : 3 * B + FB * (j + 1)]
            face_ref[j, q] = part
            high, low = halves(part)
            table_ref[q * FB : (q + 1) * FB, j * 256 : (j + 1) * 256] = high
            table_ref[(Q + q) * FB : (Q + q + 1) * FB, j * 256 : (j + 1) * 256] = low


def change_of(base_ref, cur_ref, out_ref, star_ref, fluxl_ref, fluxn_ref, wb_ref, wl_ref, s, groups):
    rows = Q * FB
    for lg in groups:
        for pair in range(2):
            cols = pl.ds((lg * 4 + 2 * pair) * LANES, 2 * LANES)
            got = mm(s["table"][...], s["hot"][:, cols])
            total = got[0:rows] + got[rows : 2 * rows]
            for half in range(2):
                s["across"][2 * pair + half] = total[:, half * LANES : (half + 1) * LANES]
        for i in range(4):
            for flux_ref, local in ((fluxl_ref, True), (fluxn_ref, False)):
                acc = [None] * Q
                for q in range(Q):
                    if local:
                        field = s["face"][i, q, :, group(lg)]
                    else:
                        field = s["across"][i, q * FB : (q + 1) * FB]
                    for p in range(Q):
                        term = flux_ref[i, p, q : q + 1, group(lg)] * field
                        acc[p] = term if acc[p] is None else acc[p] + term
                for p in range(Q):
                    high, low = halves(acc[p])
                    if local:
                        at = pl.ds(192 + i * FB, FB)
                        s["zh"][p, at, group(lg)] = high
                        s["zl"][p, at, group(lg)] = low
                    else:
                        for t in range(3):
                            at = pl.ds((3 * i + t) * FB, FB)
                            mask = s["tm"][lg, i * 3 + t]
                            s["zh"][p, at, group(lg)] = high * mask
                            s["zl"][p, at, group(lg)] = low * mask
        acc = apply_star(own_star(star_ref, lg), s["moved"], lg)
        for p in range(Q):
            out_ref[p, :, group(lg)] = base_ref[p, :, group(lg)] + acc[p]
    width = pl.ds(groups[0] * LANES, len(groups) * LANES)
    for p in range(Q):
        lifted = mm(wl_ref[...], s["zh"][p, :, width])
        rest = mm(wl_ref[0:32], s["zl"][p, :, width])
        out_ref[p, :, width] = out_ref[p, :, width] - (lifted[0:B] + lifted[32 : 32 + B] + rest[0:B])


def build_remote(stat_ref, rhot_ref, rm_ref):
    index = lax.broadcasted_iota(jnp.int32, (LANES, LANES), 0).astype(F32)
    spot, side, turn, face = (stat_ref[41, r : r + 1] for r in range(1, 5))
    segment = (lax.broadcasted_iota(jnp.int32, (1, LANES), 1) // NS * NS).astype(F32)
    spot = spot + segment
    for j in range(4):
        pick = jnp.where(side == float(j), spot, -1.0)
        rhot_ref[j * LANES : (j + 1) * LANES] = jnp.where(index == pick, 1.0, 0.0).astype(BF16)
    for i in range(4):
        for t in range(3):
            mask = jnp.where((face == float(i)) & (turn == float(t)), 1.0, 0.0).astype(F32)
            rm_ref[i * 3 + t] = jnp.broadcast_to(mask, (FB, LANES)).astype(BF16)


def project_remote(field_ref, lanes, wb_ref, table_ref):
    weights = wb_ref[3 * B - 8 :]
    for q in range(Q):
        got = mm(weights, stacked(field_ref[q, :, lanes]))
        for j in range(4):
            high, low = halves(got[8 + FB * j : 8 + FB * (j + 1)])
            table_ref[q * FB : (q + 1) * FB, j * LANES : (j + 1) * LANES] = high
            table_ref[(Q + q) * FB : (Q + q + 1) * FB, j * LANES : (j + 1) * LANES] = low


def remote_part(table_ref, stat_ref, rhot_ref, rm_ref, wl_ref, zh_ref, zl_ref):
    rows = Q * FB
    got = mm(table_ref[...], rhot_ref[...])
    across = got[0:rows] + got[rows : 2 * rows]
    acc = [None] * Q
    for q in range(Q):
        field = across[q * FB : (q + 1) * FB]
        for p in range(Q):
            term = stat_flux(stat_ref, p, q) * field
            acc[p] = term if acc[p] is None else acc[p] + term
    for p in range(Q):
        high, low = halves(acc[p])
        for c in range(12):
            zh_ref[p, c * FB : (c + 1) * FB] = high * rm_ref[c]
            zl_ref[p, c * FB : (c + 1) * FB] = low * rm_ref[c]
    out = []
    for p in range(Q):
        lifted = mm(wl_ref[:, 0:192], zh_ref[p])
        rest = mm(wl_ref[0:32, 0:192], zl_ref[p])
        out.append(lifted[0:B] + lifted[32 : 32 + B] + rest[0:B])
    return out


def pack(current_ref, other, stat_ref, msg_refs):
    blocks = []
    for p in range(Q):
        for r in range(3):
            blocks.append(current_ref[p, 8 * r : 8 * r + 8, 0:LANES])
    for p in range(Q):
        value = other(p)
        for r in range(3):
            blocks.append(value[8 * r : 8 * r + 8])
    if stat_ref is not None:
        blocks += [stat_ref[n] for n in range(STATIC)]
    while len(blocks) % 4:
        blocks.append(jnp.zeros((8, LANES), F32))
    for g in range(len(blocks) // 4):
        for k, value in enumerate(transpose_quarters(blocks[4 * g : 4 * g + 4])):
            msg_refs[k][g] = value


def unpack(msg_refs, first, last, store):
    for g in range(first // 4, -(-last // 4)):
        for m, value in enumerate(transpose_quarters([msg_refs[k][g] for k in range(4)])):
            if first <= 4 * g + m < last:
                store(4 * g + m - first, value)


def even_half(s, r, fine, dofs_ref, curo_ref, curb_ref, out_ref, msg_refs, stat_ref):
    stars = [own_star(r["star"], lg) for lg in range(2)]
    predict(dofs_ref, stars, r["wt"], s["term"], s["moved"], [(s["cur"], FIRST), (curo_ref, SECOND)])
    for p in range(Q):
        curb_ref[p] = s["cur"][p, :, 0:LANES]
    spread_and_project(s["cur"], r["wb"], s["moved"], s["face"], s["table"])
    change_of(dofs_ref, s["cur"], out_ref, r["star"], r["fluxl"], r["fluxn"], r["wb"], r["wl"], s, [0, 1])
    lead = fine[:, 0:LANES] > 0.5
    pack(
        s["cur"],
        lambda p: jnp.where(lead, out_ref[p, :, 0:LANES], curo_ref[p, :, 0:LANES]),
        stat_ref,
        msg_refs,
    )


def odd_half(s, r, fine, part_ref, curo_ref, curb_ref, recv_refs, stat_ref, ghost_ref, out_ref):
    def keep_table(n, value):
        s["gfield"][n // 3, 8 * (n % 3) : 8 * (n % 3) + 8, :] = value

    def keep_other(n, value):
        s["dofs"][n // 3, 8 * (n % 3) : 8 * (n % 3) + 8, 2 * LANES :] = value

    unpack(recv_refs, 0, 27, keep_table)
    unpack(recv_refs, 27, 54, keep_other)
    project_remote(s["gfield"], pl.ds(0, LANES), r["wb"], s["rtable"])
    project_remote(curb_ref, pl.ds(0, LANES), r["wb"], s["rtable2"])
    build_remote(stat_ref, s["rhot"], s["rm"])
    build_remote(ghost_ref, s["rhot2"], s["rm2"])
    mine = remote_part(s["rtable"], stat_ref, s["rhot"], s["rm"], r["wl"], s["rzh"], s["rzl"])
    for p in range(Q):
        s["dofs"][p, :, 0:LANES] = part_ref[p, :, 0:LANES] - mine[p]
        s["dofs"][p, :, LANES : 2 * LANES] = part_ref[p, :, LANES : 2 * LANES]
    theirs = remote_part(s["rtable2"], ghost_ref, s["rhot2"], s["rm2"], r["wl"], s["rzh"], s["rzl"])
    ghost_fine = ghost_ref[41, 5:6] > 0.5
    for p in range(Q):
        value = s["dofs"][p, :, 2 * LANES :]
        s["gfield"][p] = value
        s["dofs"][p, :, 2 * LANES :] = value - theirs[p]
    stars = [own_star(r["star"], 0), own_star(r["star"], 1), stat_star(ghost_ref)]
    predict(s["dofs"], stars, r["wt"], s["term"], s["moved"], [(s["cur"], FIRST)])
    for p in range(Q):
        s["cur"][p, :, 0:256] = jnp.where(fine > 0.5, s["cur"][p, :, 0:256], curo_ref[p])
        s["gfield"][p] = jnp.where(ghost_fine, s["cur"][p, :, 256:384], s["gfield"][p])
    project_remote(s["gfield"], pl.ds(0, LANES), r["wb"], s["rtable"])
    mine = remote_part(s["rtable"], stat_ref, s["rhot"], s["rm"], r["wl"], s["rzh"], s["rzl"])
    for p in range(Q):
        s["dofs"][p, :, 0:LANES] = s["dofs"][p, :, 0:LANES] - mine[p]
    spread_and_project(s["cur"], r["wb"], s["moved"], s["face"], s["table"])
    change_of(s["dofs"], s["cur"], out_ref, r["star"], r["fluxl"], r["fluxn"], r["wb"], r["wl"], s, [0, 1])


SCRATCH = {
    "dofs": ((Q, B, 384), F32),
    "cur": ((Q, B, 384), F32),
    "term": ((Q, B, 384), F32),
    "moved": ((Q, 3 * B, 384), F32),
    "face": ((4, Q, FB, 256), F32),
    "across": ((4, Q * FB, LANES), F32),
    "table": ((2 * Q * FB, 1024), BF16),
    "hot": ((1024, 1024), BF16),
    "tm": ((2, 12, FB, LANES), BF16),
    "zh": ((Q, 256, 256), BF16),
    "zl": ((Q, 256, 256), BF16),
}
REMOTE_SCRATCH = {
    "next": ((Q, B, 256), F32),
    "gfield": ((Q, B, LANES), F32),
    "rtable": ((2 * Q * FB, 512), BF16),
    "rtable2": ((2 * Q * FB, 512), BF16),
    "rhot": ((512, LANES), BF16),
    "rhot2": ((512, LANES), BF16),
    "rm": ((12, FB, LANES), BF16),
    "rm2": ((12, FB, LANES), BF16),
    "rzh": ((Q, 192, LANES), BF16),
    "rzl": ((Q, 192, LANES), BF16),
}


def call(kernel, name, ins, outs, scratch, inputs):
    def body(*refs):
        n, m = len(ins), len(outs)
        r = dict(zip(ins, refs[:n]))
        o = dict(zip(outs, refs[n : n + m]))
        s = dict(zip(scratch, refs[n + m :]))
        kernel(r, o, s)

    got = pl.pallas_call(
        body,
        out_shape=[jax.ShapeDtypeStruct(*outs[key]) for key in outs],
        scratch_shapes=[pltpu.VMEM(*scratch[key]) for key in scratch],
        compiler_params=pltpu.CompilerParams(vmem_limit_bytes=40 << 20),
        name=name,
    )(*(inputs[key] for key in ins))
    return dict(zip(outs, got))


def fine_of(cluster_ref):
    return (cluster_ref[...] == 0).astype(F32)


def first_kernel(r, o, s):
    prepare(
        r["time"], r["volume"], r["project"], r["rotate"], r["lift"],
        o["wt"], o["wb"], o["wl"], s["ptmp"], s["pbig"],
    )
    describe(r["nbr"], r["kind"], r["cluster"], r["star"], r["fluxn"], o["stat"])
    for p in range(Q):
        s["dofs"][p, 0:20, 0:256] = r["dofs"][p]
        s["dofs"][p, 20:B, 0:256] = jnp.zeros((B - 20, 256), F32)
    build_onehot(r["nbr"], r["kind"], s["hot"], s["tm"], [0, 1])
    r = dict(r, wt=o["wt"], wb=o["wb"], wl=o["wl"])
    msgs = [o["m%d" % k] for k in range(4)]
    even_half(s, r, fine_of(r["cluster"]), s["dofs"], o["curo"], o["curb"], o["part"], msgs, o["stat"])


def middle_kernel(r, o, s):
    build_onehot(r["nbr"], r["kind"], s["hot"], s["tm"], [0, 1])
    recv = [r["r%d" % k] for k in range(4)]

    def keep(n, value):
        o["ghost"][n] = value

    unpack(recv, 54, 54 + STATIC, keep)
    fine = fine_of(r["cluster"])
    odd_half(s, r, fine, r["part"], r["curo"], r["curb"], recv, r["stat"], o["ghost"], s["next"])
    msgs = [o["m%d" % k] for k in range(4)]
    even_half(s, r, fine, s["next"], o["curo"], o["curb"], o["part"], msgs, None)


def last_kernel(r, o, s):
    build_onehot(r["nbr"], r["kind"], s["hot"], s["tm"], [0, 1])
    recv = [r["r%d" % k] for k in range(4)]
    odd_half(s, r, fine_of(r["cluster"]), r["part"], r["curo"], r["curb"], recv, r["stat"], r["ghost"], s["next"])
    for p in range(Q):
        o["out"][p] = s["next"][p, 0:20, :]


def trade(got):
    lines = (("px", 1), ("px", -1), ("py", 1), ("py", -1))
    out = {}
    for k, (axis, step) in enumerate(lines):
        count = lax.axis_size(axis)
        if step > 0:
            pairs = [(i, i + 1) for i in range(count - 1)]
        else:
            pairs = [(i + 1, i) for i in range(count - 1)]
        out["r%d" % k] = lax.ppermute(got["m%d" % (k ^ 1)], axis, pairs)
    return out


def per_device(dofs, star, flux_local, flux_neigh, time_stiff, volume_stiff, face_project, face_rotate, face_lift, cluster, neighbors, face_kind):
    inputs = dict(
        dofs=dofs, star=star, fluxl=flux_local, fluxn=flux_neigh, time=time_stiff, volume=volume_stiff,
        project=face_project, rotate=face_rotate, lift=face_lift,
        cluster=cluster.reshape(1, 256), nbr=neighbors, kind=face_kind,
    )
    field = ((Q, B, 256), F32)
    state = {"part": field, "curo": field, "curb": ((Q, B, LANES), F32)}
    first = {
        **state,
        "wt": ((80, 80), BF16),
        "wb": ((144, 80), BF16),
        "wl": ((64, 256), BF16),
        "stat": ((STATIC, 8, LANES), F32),
        **{"m%d" % k: ((24, 8, LANES), F32) for k in range(4)},
    }
    got = call(
        first_kernel, "first", list(inputs), first,
        {**SCRATCH, "ptmp": ((144, 80), F32), "pbig": ((64, 256), F32)}, inputs,
    )
    inputs |= got
    inputs |= trade(got)
    shared = ["star", "fluxl", "fluxn", "wt", "wb", "wl", "cluster", "nbr", "kind", "stat", "part", "curo", "curb"]
    shared += ["r%d" % k for k in range(4)]
    middle = {
        **state,
        "ghost": ((STATIC, 8, LANES), F32),
        **{"m%d" % k: ((14, 8, LANES), F32) for k in range(4)},
    }
    got = call(middle_kernel, "middle", shared, middle, {**SCRATCH, **REMOTE_SCRATCH}, inputs)
    inputs |= got
    inputs |= trade(got)
    got = call(
        last_kernel, "last", shared + ["ghost"], {"out": ((Q, 20, 256), F32)},
        {**SCRATCH, **REMOTE_SCRATCH}, inputs,
    )
    return got["out"]


def solution(mesh):
    cells = ("px", "py")
    placed = (
        P(None, None, cells),
        P(None, None, None, cells),
        P(None, None, None, cells),
        P(None, None, None, cells),
        P(),
        P(),
        P(),
        P(),
        P(),
        P(cells),
        P(None, cells),
        P(None, cells),
    )
    return jax.shard_map(
        per_device,
        mesh=mesh,
        in_specs=placed,
        out_specs=P(None, None, cells),
        check_vma=False,
    )
```

profile of v0, /device:TPU:129, one launch (start us, length us, event | category | flops | bytes accessed | tf_op | source)
XLA Modules:
  0.0 68.6 jit_solution(7962077684421080532)
XLA Ops:
  0.0 0.0 copy-start.8
  0.0 0.7 %copy.17.refs_7_ = f32[3,10,10]{2,1,0:T(8,128)S(1)} copy(f32[3,10,10]{2,0,1:T(4,128)} %param.19) | data formatting | bytes 2400 | tf_op args[7]
  0.7 0.0 copy-done.8
  0.7 0.0 copy-start.9
  0.8 0.7 %copy-done.9 = f32[4,20,10]{1,0,2:T(4,128)S(1)} copy-done((f32[4,20,10]{1,0,2:T(4,128)S(1)}, f32[4,20,10]{1,0,2:T(4,128)}, u32[]{:S(2)}) %copy-start.9) | copy-done | bytes 3224
  1.5 0.1 copy.18.refs_8_
  1.6 0.0 copy-start.6
  1.6 1.1 %copy.22.refs_1_.refs_0_ = f32[3,9,9,256]{3,2,1,0:T(8,128)S(1)} copy(f32[3,9,9,256]{3,0,2,1:T(4,128)} %param.13) | data formatting | bytes 497664 | tf_op args[1]
  2.7 0.0 copy-done.6
  2.7 0.0 copy-start.7
  2.7 0.1 copy.23.refs_2_.refs_1_
  2.8 0.9 %copy-done.7 = f32[4,9,9,256]{3,0,2,1:T(4,128)S(1)} copy-done((f32[4,9,9,256]{3,0,2,1:T(4,128)S(1)}, f32[4,9,9,256]{3,0,2,1:T(4,128)}, u32[]{:S(2)}) %copy-start.7) | copy-done | bytes 331800
  3.7 0.0 copy-start
  3.7 0.0 copy-start.1
  3.7 0.0 copy-start.2
  3.7 0.0 copy-start.3
  3.7 0.0 copy-start.4
  3.7 0.1 copy.24.refs_3_.refs_2_
  3.8 0.0 copy-start.5
  3.8 0.8 %copy-done = f32[9,20,256]{2,1,0:T(8,128)S(1)} copy-done((f32[9,20,256]{2,1,0:T(8,128)S(1)}, f32[9,20,256]{2,1,0:T(8,128)}, u32[]{:S(2)}) %copy-start) | copy-done | bytes 184344
  4.6 0.0 copy-done.1
  4.6 0.0 copy-done.2
  4.6 0.0 copy-done.3
  4.6 0.0 copy-done.4
  4.6 0.0 copy-done.5
  4.6 6.9 %first.1 = (f32[9,24,256]{2,1,0:T(8,128)S(1)}, f32[9,24,256]{2,1,0:T(8,128)S(1)}, f32[9,24,128]{2,1,0:T(8,128)S(1)}, bf16[80,80]{1,0:T(8,128)(2,1)S(1)}, bf16[14...) custom-call(f32[9,20,256]{2,1,0:T(8,128)S(1)} %copy-done, ...), custom_call_target="tpu_custom_call" | custom-call | tf_op jit(solution)/shard_map/first/pallas_call | solution.py:422
  11.6 3.2 %collective-permute-start = (f32[24,8,128]{2,1,0:T(8,128)S(1)}, f32[24,8,128]{2,1,0:T(8,128)S(1)}, u32[]{:S(2)}, u32[]{:S(2)}) collective-permute-start(f32[24,8,128]{2,1,0:T(8,128)S(1)} %get-tuple-element.31), channel_id=1, source_target_pairs={{0,8},{8,16},{16,24},{24,32},{32,40},{40,48},{48,56},{56,64},{64,7... | collective-permute-start | bytes 294920 | tf_op jit(solution)/shard_map/ppermute | solution.py:482
  14.8 5.4 %collective-permute-start.1 = (f32[24,8,128]{2,1,0:T(8,128)S(1)}, f32[24,8,128]{2,1,0:T(8,128)S(1)}, u32[]{:S(2)}, u32[]{:S(2)}) collective-permute-start(f32[24,8,128]{2,1,0:T(8,128)S(1)} %get-tuple-element.32), channel_id=1, source_target_pairs={{8,0},{16,8},{24,16},{32,24},{40,32},{48,40},{56,48},{64,56},{72,6... | collective-permute-start | bytes 294920 | tf_op jit(solution)/shard_map/ppermute | solution.py:482
  20.2 4.2 %collective-permute-start.2 = (f32[24,8,128]{2,1,0:T(8,128)S(1)}, f32[24,8,128]{2,1,0:T(8,128)S(1)}, u32[]{:S(2)}, u32[]{:S(2)}) collective-permute-start(f32[24,8,128]{2,1,0:T(8,128)S(1)} %get-tuple-element.33), channel_id=1, source_target_pairs={{0,1},{1,2},{2,3},{3,4},{4,5},{5,6},{6,7},{8,9},{9,10},{10,11},{11... | collective-permute-start | bytes 294920 | tf_op jit(solution)/shard_map/ppermute | solution.py:482
  24.4 2.1 %collective-permute-start.3 = (f32[24,8,128]{2,1,0:T(8,128)S(1)}, f32[24,8,128]{2,1,0:T(8,128)S(1)}, u32[]{:S(2)}, u32[]{:S(2)}) collective-permute-start(f32[24,8,128]{2,1,0:T(8,128)S(1)} %get-tuple-element.34), channel_id=1, source_target_pairs={{1,0},{2,1},{3,2},{4,3},{5,4},{6,5},{7,6},{9,8},{10,9},{11,10},{12... | collective-permute-start | bytes 294920 | tf_op jit(solution)/shard_map/ppermute | solution.py:482
  26.5 0.0 collective-permute-done.refs_13_
  26.5 0.0 collective-permute-done.1.refs_14_
  26.6 0.0 collective-permute-done.2.refs_15_
  26.6 3.8 %collective-permute-done.3.refs_16_ = f32[24,8,128]{2,1,0:T(8,128)S(1)} collective-permute-done((f32[24,8,128]{2,1,0:T(8,128)S(1)}, f32[24,8,128]{2,1,0:T(8,128)S(1)}, u32[]{:S(2)}, u32[]{:S(2)}) %collective-permute-start.3) | collective-permute-done | bytes 98336 | tf_op jit(solution)/shard_map/ppermute | solution.py:482
  30.4 12.7 %middle.1 = (f32[9,24,256]{2,1,0:T(8,128)S(1)}, f32[9,24,256]{2,1,0:T(8,128)S(1)}, f32[9,24,128]{2,1,0:T(8,128)S(1)}, f32[42,8,128]{2,1,0:T(8,128)S(1)}, f32[14,...) custom-call(f32[3,9,9,256]{3,2,1,0:T(8,128)S(1)} %copy.22.refs_1_.refs_0_, ...), custom_call_target="tpu_custom_call" | custom-call | tf_op jit(solution)/shard_map/middle/pallas_call | solution.py:422
  43.1 1.9 %collective-permute-start.4 = (f32[14,8,128]{2,1,0:T(8,128)S(1)}, f32[14,8,128]{2,1,0:T(8,128)S(1)}, u32[]{:S(2)}, u32[]{:S(2)}) collective-permute-start(f32[14,8,128]{2,1,0:T(8,128)S(1)} %get-tuple-element.38), channel_id=1, source_target_pairs={{0,8},{8,16},{16,24},{24,32},{32,40},{40,48},{48,56},{56,64},{64,7... | collective-permute-start | bytes 172040 | tf_op jit(solution)/shard_map/ppermute | solution.py:482
  45.0 6.7 %collective-permute-start.5 = (f32[14,8,128]{2,1,0:T(8,128)S(1)}, f32[14,8,128]{2,1,0:T(8,128)S(1)}, u32[]{:S(2)}, u32[]{:S(2)}) collective-permute-start(f32[14,8,128]{2,1,0:T(8,128)S(1)} %get-tuple-element.39), channel_id=1, source_target_pairs={{8,0},{16,8},{24,16},{32,24},{40,32},{48,40},{56,48},{64,56},{72,6... | collective-permute-start | bytes 172040 | tf_op jit(solution)/shard_map/ppermute | solution.py:482
  51.7 2.4 %collective-permute-start.6 = (f32[14,8,128]{2,1,0:T(8,128)S(1)}, f32[14,8,128]{2,1,0:T(8,128)S(1)}, u32[]{:S(2)}, u32[]{:S(2)}) collective-permute-start(f32[14,8,128]{2,1,0:T(8,128)S(1)} %get-tuple-element.40), channel_id=1, source_target_pairs={{0,1},{1,2},{2,3},{3,4},{4,5},{5,6},{6,7},{8,9},{9,10},{10,11},{11... | collective-permute-start | bytes 172040 | tf_op jit(solution)/shard_map/ppermute | solution.py:482
  54.1 2.1 %collective-permute-start.7 = (f32[14,8,128]{2,1,0:T(8,128)S(1)}, f32[14,8,128]{2,1,0:T(8,128)S(1)}, u32[]{:S(2)}, u32[]{:S(2)}) collective-permute-start(f32[14,8,128]{2,1,0:T(8,128)S(1)} %get-tuple-element.41), channel_id=1, source_target_pairs={{1,0},{2,1},{3,2},{4,3},{5,4},{6,5},{7,6},{9,8},{10,9},{11,10},{12... | collective-permute-start | bytes 172040 | tf_op jit(solution)/shard_map/ppermute | solution.py:482
  56.3 0.0 collective-permute-done.4.refs_13_
  56.3 0.0 collective-permute-done.5.refs_14_
  56.3 0.0 collective-permute-done.6.refs_15_
  56.3 3.3 %collective-permute-done.7.refs_16_ = f32[14,8,128]{2,1,0:T(8,128)S(1)} collective-permute-done((f32[14,8,128]{2,1,0:T(8,128)S(1)}, f32[14,8,128]{2,1,0:T(8,128)S(1)}, u32[]{:S(2)}, u32[]{:S(2)}) %collective-permute-start.7) | collective-permute-done | bytes 57376 | tf_op jit(solution)/shard_map/ppermute | solution.py:482
  59.6 8.9 %last.1 = f32[9,20,256]{2,1,0:T(8,128)} custom-call(f32[3,9,9,256]{3,2,1,0:T(8,128)S(1)} %copy.22.refs_1_.refs_0_, f32[4,9,9,256]{3,2,1,0:T(8,128)S(1)} %copy.23.refs_2_.refs_1_, f32[4,9,9,256]{3,2,1,0:T(8,128)S(1)} %copy.24.refs_3_.refs_2_, bf16[80,80]{1,0:T(8,128)(2,1)S(1)} %get-tuple-element.24.refs_3_, bf16[144,80]{1,0:T(8,128)(2,1)S(1)} %get-tuple-element.25.refs_4_, ...), custom_call_target="tpu_custom_call" | custom-call | tf_op jit(solution)/shard_map/last/pallas_call | solution.py:422
  (1 shorter events, 0.0 us)
Async XLA Ops:
  0.0 0.7 %copy-start.8 = (f32[4,10,20]{2,0,1:T(4,128)S(1)}, f32[4,10,20]{2,0,1:T(4,128)}, u32[]{:S(2)}) copy-start(f32[4,10,20]{2,0,1:T(4,128)} %param.18) | copy-start | bytes 9604
  0.7 0.7 %copy-start.9 = (f32[4,20,10]{1,0,2:T(4,128)S(1)}, f32[4,20,10]{1,0,2:T(4,128)}, u32[]{:S(2)}) copy-start(f32[4,20,10]{1,0,2:T(4,128)} %param.20) | copy-start | bytes 9604
  1.6 1.1 %copy-start.6 = (f32[4,9,9,256]{3,0,2,1:T(4,128)S(1)}, f32[4,9,9,256]{3,0,2,1:T(4,128)}, u32[]{:S(2)}) copy-start(f32[4,9,9,256]{3,0,2,1:T(4,128)} %param.14) | copy-start | bytes 995332
  2.7 1.0 %copy-start.7 = (f32[4,9,9,256]{3,0,2,1:T(4,128)S(1)}, f32[4,9,9,256]{3,0,2,1:T(4,128)}, u32[]{:S(2)}) copy-start(f32[4,9,9,256]{3,0,2,1:T(4,128)} %param.15) | copy-start | bytes 995332
  3.7 0.9 %copy-start = (f32[9,20,256]{2,1,0:T(8,128)S(1)}, f32[9,20,256]{2,1,0:T(8,128)}, u32[]{:S(2)}) copy-start(f32[9,20,256]{2,1,0:T(8,128)} %refs_0_.3) | copy-start | bytes 552964
  3.7 0.9 %copy-start.1 = (f32[3,20,20]{2,1,0:T(8,128)S(1)}, f32[3,20,20]{2,1,0:T(8,128)}, u32[]{:S(2)}) copy-start(f32[3,20,20]{2,1,0:T(8,128)} %refs_4_.1) | copy-start | bytes 14404
  3.7 0.9 %copy-start.2 = (f32[3,20,20]{2,1,0:T(8,128)S(1)}, f32[3,20,20]{2,1,0:T(8,128)}, u32[]{:S(2)}) copy-start(f32[3,20,20]{2,1,0:T(8,128)} %refs_5_.1) | copy-start | bytes 14404
  3.7 0.9 %copy-start.3 = (s32[4,256]{1,0:T(4,128)S(1)}, s32[4,256]{1,0:T(4,128)}, u32[]{:S(2)}) copy-start(s32[4,256]{1,0:T(4,128)} %refs_7_.4) | copy-start | bytes 12292
  3.7 0.9 %copy-start.4 = (s32[4,256]{1,0:T(4,128)S(1)}, s32[4,256]{1,0:T(4,128)}, u32[]{:S(2)}) copy-start(s32[4,256]{1,0:T(4,128)} %refs_8_.4) | copy-start | bytes 12292
  3.8 0.8 %copy-start.5 = (s32[256]{0:T(256)S(1)}, s32[256]{0:T(256)}, u32[]{:S(2)}) copy-start(s32[256]{0:T(256)} %param.21) | copy-start | bytes 3076
  11.6 15.0 %collective-permute-start = (f32[24,8,128]{2,1,0:T(8,128)S(1)}, f32[24,8,128]{2,1,0:T(8,128)S(1)}, u32[]{:S(2)}, u32[]{:S(2)}) collective-permute-start(f32[24,8,128]{2,1,0:T(8,128)S(1)} %get-tuple-element.31), channel_id=1, source_target_pairs={{0,8},{8,16},{16,24},{24,32},{32,40},{40,48},{48,56},{56,64},{64,7... | collective-permute-start | bytes 294920 | tf_op jit(solution)/shard_map/ppermute | solution.py:482
  14.8 11.8 %collective-permute-start.1 = (f32[24,8,128]{2,1,0:T(8,128)S(1)}, f32[24,8,128]{2,1,0:T(8,128)S(1)}, u32[]{:S(2)}, u32[]{:S(2)}) collective-permute-start(f32[24,8,128]{2,1,0:T(8,128)S(1)} %get-tuple-element.32), channel_id=1, source_target_pairs={{8,0},{16,8},{24,16},{32,24},{40,32},{48,40},{56,48},{64,56},{72,6... | collective-permute-start | bytes 294920 | tf_op jit(solution)/shard_map/ppermute | solution.py:482
  20.2 6.4 %collective-permute-start.2 = (f32[24,8,128]{2,1,0:T(8,128)S(1)}, f32[24,8,128]{2,1,0:T(8,128)S(1)}, u32[]{:S(2)}, u32[]{:S(2)}) collective-permute-start(f32[24,8,128]{2,1,0:T(8,128)S(1)} %get-tuple-element.33), channel_id=1, source_target_pairs={{0,1},{1,2},{2,3},{3,4},{4,5},{5,6},{6,7},{8,9},{9,10},{10,11},{11... | collective-permute-start | bytes 294920 | tf_op jit(solution)/shard_map/ppermute | solution.py:482
  24.4 5.9 %collective-permute-start.3 = (f32[24,8,128]{2,1,0:T(8,128)S(1)}, f32[24,8,128]{2,1,0:T(8,128)S(1)}, u32[]{:S(2)}, u32[]{:S(2)}) collective-permute-start(f32[24,8,128]{2,1,0:T(8,128)S(1)} %get-tuple-element.34), channel_id=1, source_target_pairs={{1,0},{2,1},{3,2},{4,3},{5,4},{6,5},{7,6},{9,8},{10,9},{11,10},{12... | collective-permute-start | bytes 294920 | tf_op jit(solution)/shard_map/ppermute | solution.py:482
  43.1 13.2 %collective-permute-start.4 = (f32[14,8,128]{2,1,0:T(8,128)S(1)}, f32[14,8,128]{2,1,0:T(8,128)S(1)}, u32[]{:S(2)}, u32[]{:S(2)}) collective-permute-start(f32[14,8,128]{2,1,0:T(8,128)S(1)} %get-tuple-element.38), channel_id=1, source_target_pairs={{0,8},{8,16},{16,24},{24,32},{32,40},{40,48},{48,56},{56,64},{64,7... | collective-permute-start | bytes 172040 | tf_op jit(solution)/shard_map/ppermute | solution.py:482
  45.0 11.3 %collective-permute-start.5 = (f32[14,8,128]{2,1,0:T(8,128)S(1)}, f32[14,8,128]{2,1,0:T(8,128)S(1)}, u32[]{:S(2)}, u32[]{:S(2)}) collective-permute-start(f32[14,8,128]{2,1,0:T(8,128)S(1)} %get-tuple-element.39), channel_id=1, source_target_pairs={{8,0},{16,8},{24,16},{32,24},{40,32},{48,40},{56,48},{64,56},{72,6... | collective-permute-start | bytes 172040 | tf_op jit(solution)/shard_map/ppermute | solution.py:482
  51.7 4.6 %collective-permute-start.6 = (f32[14,8,128]{2,1,0:T(8,128)S(1)}, f32[14,8,128]{2,1,0:T(8,128)S(1)}, u32[]{:S(2)}, u32[]{:S(2)}) collective-permute-start(f32[14,8,128]{2,1,0:T(8,128)S(1)} %get-tuple-element.40), channel_id=1, source_target_pairs={{0,1},{1,2},{2,3},{3,4},{4,5},{5,6},{6,7},{8,9},{9,10},{10,11},{11... | collective-permute-start | bytes 172040 | tf_op jit(solution)/shard_map/ppermute | solution.py:482
  54.1 5.5 %collective-permute-start.7 = (f32[14,8,128]{2,1,0:T(8,128)S(1)}, f32[14,8,128]{2,1,0:T(8,128)S(1)}, u32[]{:S(2)}, u32[]{:S(2)}) collective-permute-start(f32[14,8,128]{2,1,0:T(8,128)S(1)} %get-tuple-element.41), channel_id=1, source_target_pairs={{1,0},{2,1},{3,2},{4,3},{5,4},{6,5},{7,6},{9,8},{10,9},{11,10},{12... | collective-permute-start | bytes 172040 | tf_op jit(solution)/shard_map/ppermute | solution.py:482
where the time goes:
time: 69 us; the launch traced here: 68.6 us
  Pallas kernels  28.6 us (41%)
  starting transfers between devices  28.1 us (41%)
  waiting for transfers between devices  7.12 us (10%)
  local copies, waits for them, and re-layouts  4.56 us (7%)
    pallas_call x3, Pallas kernels, call(): pl.pallas_call(body, out_shape=[jax.ShapeDtypeStruct(*outs[key]) for key...  28.6 us
    ppermute x8, starting transfers between devices, trade(): out['r%d' % k] = lax.ppermute(got['m%d' % (k ^ 1)], axis, pairs)  28.1 us
    ppermute x8, waiting for transfers between devices, trade(): out['r%d' % k] = lax.ppermute(got['m%d' % (k ^ 1)], axis, pairs)  7.12 us
    unnamed x26, local copies, waits for them, and re-layouts  4.56 us
  transfers between devices with their start and end apart: 8, of which 2 were waited for; matrix products, arithmetic and copies ran while one was open for 0% of the time, Pallas kernels for 0%

commit v1 on v0

v1 whole, which is shorter than its diff:
```python
import math
from functools import partial

import jax
import jax.numpy as jnp
from jax import lax
from jax.experimental import pallas as pl
from jax.experimental.pallas import tpu as pltpu
from jax.sharding import PartitionSpec as P

ORDER = 4
NS = 32
Q = 9
B = 24
FB = 16
LANES = 128
KZ = 160
STATIC = 42
F32 = jnp.float32
BF16 = jnp.bfloat16
HIGHEST = lax.Precision.HIGHEST
STEP = 0.4
SENT = ("m0", "m1", "m2", "m3")
GOT = ("r0", "r1", "r2", "r3")


class Bag(dict):
    __getattr__ = dict.__getitem__
    __setattr__ = dict.__setitem__

    def __or__(self, other):
        return Bag({**self, **other})

    def pick(self, name, lg):
        return self[name + str(lg)]


def series(start, stop):
    return [
        (stop ** (power + 1) - start ** (power + 1)) / math.factorial(power + 1)
        for power in range(ORDER)
    ]


FIRST = series(0.0, STEP)
SECOND = series(STEP, 2.0 * STEP)


def halves(x):
    high = x.astype(BF16)
    return high, (x - high.astype(F32)).astype(BF16)


def stacked(x):
    high = x.astype(BF16).astype(F32)
    rest = jnp.zeros((8, x.shape[1]), F32)
    return jnp.concatenate([high, x - high, high, rest], axis=0).astype(BF16)


def mm(a, b):
    return jnp.dot(a, b, preferred_element_type=F32)


def group(lg):
    return pl.ds(lg * LANES, LANES)


def transpose_quarters(four):
    quarter = lax.broadcasted_iota(jnp.int32, (8, LANES), 1) // NS
    out = []
    for k in range(4):
        total = None
        for m in range(4):
            shift = (NS * (m - k)) % LANES
            moved = pltpu.roll(four[m], shift, 1) if shift else four[m]
            total = moved if total is None else jnp.where(quarter == m, moved, total)
        out.append(total)
    return out


def widened(block):
    high = block.astype(BF16).astype(F32)
    return (high + pltpu.roll(high, B, 1) + pltpu.roll(block - high, 2 * B, 1)).astype(BF16)


def prepare_predictor(time_ref, wt_ref, tmp_ref):
    tmp_ref[...] = jnp.zeros_like(tmp_ref)
    for d in range(3):
        tmp_ref[B * d : B * d + 20, 0:20] = -time_ref[d]
    wt_ref[...] = widened(tmp_ref[0:80])[:, 0:80]


def prepare(volume_ref, project_ref, rotate_ref, lift_ref, wb_ref, wl_ref, tmp_ref, turn_ref, big_ref):
    for d in range(3):
        tmp_ref[B * d : B * d + 20, 0:20] = volume_ref[d]
    for j in range(4):
        at = 3 * B + FB * j
        tmp_ref[at : at + 8, 0:20] = project_ref[0:8, j, :]
        for r in range(4):
            tmp_ref[at + 8 + r : at + 9 + r, 0:20] = project_ref[8:9, j, :]
            tmp_ref[at + 12 + r : at + 13 + r, 0:20] = project_ref[9:10, j, :]
    wb_ref[...] = widened(tmp_ref[...])[:, 0:80]
    turn_ref[...] = jnp.zeros_like(turn_ref)
    for t in range(3):
        turn_ref[0:10, FB * t : FB * t + 10] = rotate_ref[:, t, :]
    rows = lax.broadcasted_iota(jnp.int32, (10, 10), 0)
    cols = lax.broadcasted_iota(jnp.int32, (10, 10), 1)
    turn_ref[0:10, 3 * FB : 3 * FB + 10] = (rows == cols).astype(F32)
    turns = turn_ref[...].T[0:64, 0:16]
    big_ref[...] = jnp.zeros_like(big_ref)
    for i in range(4):
        big_ref[0:10, 32 * i : 32 * i + 20] = lift_ref[:, i, :]
    both = jnp.dot(turns, big_ref[0:16], precision=HIGHEST, preferred_element_type=F32)
    big_ref[0:16] = jnp.zeros((16, LANES), F32)
    for i in range(4):
        mine = pltpu.roll(both, LANES - 32 * i, 1) if i else both
        for t in range(4):
            at = (((i // 2) * 3 + t) if t < 3 else 6 + i // 2) * FB + 8 * (i % 2)
            big_ref[at : at + 8] = mine[FB * t : FB * t + 8]
            for g in (8, 9):
                at = 128 + 8 * t + 4 * (g - 8) + i
                big_ref[at : at + 1] = mine[FB * t + g : FB * t + g + 1]
    total = big_ref[...].T[0:32, 0:KZ]
    high = total.astype(BF16).astype(F32)
    wl_ref[...] = jnp.concatenate([high, total - high], axis=0).astype(BF16)


def describe(nbr_ref, kind_ref, cluster_ref, star_ref, fluxn_ref, stat_ref):
    lanes = pl.ds(0, LANES)
    here = nbr_ref[0:1, LANES : 2 * LANES] >> 8
    remote = []
    for i in range(4):
        nbr = nbr_ref[i : i + 1, lanes]
        remote.append((nbr >= 0) & ((nbr >> 8) != here))
    spot = jnp.full((1, LANES), -1, jnp.int32)
    side = jnp.full((1, LANES), -1, jnp.int32)
    turn = jnp.full((1, LANES), -1, jnp.int32)
    face = jnp.full((1, LANES), -1, jnp.int32)
    for i in range(4):
        kind = kind_ref[i : i + 1, lanes]
        spot = jnp.where(remote[i], nbr_ref[i : i + 1, lanes] & (NS - 1), spot)
        side_i = (kind >= 3).astype(jnp.int32) + (kind >= 6).astype(jnp.int32) + (kind >= 9).astype(jnp.int32)
        side = jnp.where(remote[i], side_i, side)
        turn = jnp.where(remote[i], kind - 3 * side_i, turn)
        face = jnp.where(remote[i], i, face)
    weight = [jnp.where(r, 1.0, 0.0).astype(F32) for r in remote]
    stat_ref[27 + 3] = jnp.zeros((8, LANES), F32)
    for d in range(3):
        for p in range(Q):
            at = d * Q + p
            stat_ref[at] = star_ref[p, 0:8, d, lanes]
            stat_ref[27 + at // 8, at % 8 : at % 8 + 1] = star_ref[p, 8, d : d + 1, lanes]
    stat_ref[41] = jnp.zeros((8, LANES), F32)
    for p in range(Q):
        total, last = None, None
        for i in range(4):
            term = fluxn_ref[p, 0:8, i, lanes] * weight[i]
            term_last = fluxn_ref[p, 8, i : i + 1, lanes] * weight[i]
            total = term if total is None else total + term
            last = term_last if last is None else last + term_last
        stat_ref[31 + p] = total
        stat_ref[40 + p // 8, p % 8 : p % 8 + 1] = last
    fine = (cluster_ref[0:1, lanes] == 0).astype(F32)
    for row, value in enumerate((spot.astype(F32), side.astype(F32), turn.astype(F32), face.astype(F32), fine)):
        stat_ref[41, row + 1 : row + 2] = value


def stat_star(stat_ref):
    def at(d, p, q):
        n = d * Q + p
        return stat_ref[n, q : q + 1] if q < 8 else stat_ref[27 + n // 8, n % 8 : n % 8 + 1]

    return at


def stat_flux(stat_ref, p, q):
    return stat_ref[31 + p, q : q + 1] if q < 8 else stat_ref[40 + p // 8, p % 8 : p % 8 + 1]


def own_star(star_ref, lg):
    return lambda d, p, q: star_ref[p, q, d : d + 1, group(lg)]


def apply_star(star, moved_ref, lanes):
    acc = [None] * Q
    for q in range(Q):
        for d in range(3):
            field = moved_ref[q, B * d : B * d + B, lanes]
            for p in range(Q):
                term = star(d, p, q) * field
                acc[p] = term if acc[p] is None else acc[p] + term
    return acc


def predict(dofs_ref, stars, wt_ref, term_ref, moved_ref, outs):
    width = LANES * len(stars)
    for power in range(ORDER - 1):
        source = term_ref if power else dofs_ref
        for q in range(Q):
            moved_ref[q, 0 : 3 * B, 0:width] = mm(wt_ref[...], stacked(source[q, :, 0:width]))[0 : 3 * B]
        for lg, star in enumerate(stars):
            acc = apply_star(star, moved_ref, group(lg))
            for p in range(Q):
                if power < ORDER - 2:
                    term_ref[p, :, group(lg)] = acc[p]
                for out_ref, coeffs in outs:
                    before = out_ref[p, :, group(lg)] if power else coeffs[0] * dofs_ref[p, :, group(lg)]
                    out_ref[p, :, group(lg)] = before + coeffs[power + 1] * acc[p]


def keep_masks(test, pair_ref, last_ref):
    for t in range(3):
        mask = [jnp.where(test(i, t), 1.0, 0.0).astype(F32) for i in range(4)]
        for pair in range(2):
            two = [jnp.broadcast_to(mask[2 * pair + n], (8, LANES)) for n in range(2)]
            pair_ref[pair * 3 + t] = jnp.concatenate(two, axis=0).astype(BF16)
        last_ref[t] = by_face(mask)


def by_face(four):
    which = lax.broadcasted_iota(jnp.int32, (8, LANES), 0) & 3
    total = jnp.broadcast_to(four[0], (8, LANES))
    for i in range(1, 4):
        total = jnp.where(which == i, four[i], total)
    return total


def keep_rows(flux_ref, lg, rows_ref):
    for p in range(Q):
        for q in range(Q):
            tile = flux_ref[p, q, :, group(lg)]
            rows_ref[p * Q + q, 0:4] = tile
            rows_ref[p * Q + q, 4:8] = tile


def fill_z(p, lanes, mains, last, pair_ref, last_ref, zh_ref, zl_ref):
    for pair in range(2):
        high, low = halves(jnp.concatenate(mains[2 * pair : 2 * pair + 2], axis=0))
        for t in range(3):
            at = pl.ds((pair * 3 + t) * FB, FB)
            zh_ref[p, at, lanes] = high * pair_ref[pair * 3 + t]
            zl_ref[p, at, lanes] = low * pair_ref[pair * 3 + t]
    return [last * last_ref[t] for t in range(3)]


def finish_z(p, lanes, turned, local, zh_ref, zl_ref):
    for n, two in enumerate(((turned[0], turned[1]), (turned[2], local))):
        high, low = halves(jnp.concatenate(two, axis=0))
        zh_ref[p, 128 + n * FB : 128 + (n + 1) * FB, lanes] = high
        zl_ref[p, 128 + n * FB : 128 + (n + 1) * FB, lanes] = low


def build_onehot(nbr_ref, kind_ref, s, groups):
    index = lax.broadcasted_iota(jnp.int32, (256, LANES), 0)
    here = nbr_ref[0:1, LANES : 2 * LANES] >> 8
    for lg in groups:
        turns = []
        for i in range(4):
            nbr = nbr_ref[i : i + 1, group(lg)]
            kind = kind_ref[i : i + 1, group(lg)]
            local = (nbr >= 0) & ((nbr >> 8) == here)
            side = (kind >= 3).astype(jnp.int32) + (kind >= 6).astype(jnp.int32) + (kind >= 9).astype(jnp.int32)
            turn = kind - 3 * side
            for j in range(4):
                pick = jnp.where(local & (side == j), nbr & 255, -1)
                hot = jnp.where(index == pick, 1.0, 0.0).astype(BF16)
                s.pick("hot", lg)[j * 256 : (j + 1) * 256, group(i)] = hot
            turns.append(turn)
        keep_masks(lambda i, t: turns[i] == t, s.pick("tm", lg), s.pick("um", lg))


def spread_and_project(cur_ref, wb_ref, s):
    for q in range(Q):
        got = mm(wb_ref[...], stacked(cur_ref[q, :, 0:256]))
        for lg in range(2):
            half = got[:, lg * LANES : (lg + 1) * LANES]
            s.pick("moved", lg)[q] = half[0 : 3 * B]
            for j in range(4):
                s.pick("face", lg)[j, q] = half[3 * B + FB * j : 3 * B + FB * (j + 1)]
        for j in range(4):
            high, low = halves(got[3 * B + FB * j : 3 * B + FB * (j + 1)])
            s.table[q * FB : (q + 1) * FB, j * 256 : (j + 1) * 256] = high
            s.table[(Q + q) * FB : (Q + q + 1) * FB, j * 256 : (j + 1) * 256] = low


def change_of(base, out, r, s, groups):
    rows = Q * FB
    for lg in groups:
        at_lg = group(groups.index(lg))
        for pair in range(2):
            cols = pl.ds(2 * pair * LANES, 2 * LANES)
            got = mm(s.table[...], s.pick("hot", lg)[:, cols])
            total = got[0:rows] + got[rows : 2 * rows]
            for half in range(2):
                s.across[2 * pair + half] = total[:, half * LANES : (half + 1) * LANES]
        face, across = s.pick("face", lg), s.across
        sources = (
            (r.fluxl, s.pick("fpl", lg), lambda i, q, rows: face[i, q, rows]),
            (r.fluxn, s.pick("fpn", lg), lambda i, q, rows: across[i, q * FB + rows.start : q * FB + rows.stop]),
        )
        got = []
        for flux_ref, rows_ref, field in sources:
            sums = []
            for i in range(5):
                acc = [None] * Q
                for q in range(Q):
                    if i < 4:
                        value = field(i, q, slice(0, 8))
                    else:
                        value = by_face([field(k, q, slice(8, 16)) for k in range(4)])
                    for p in range(Q):
                        scale = flux_ref[p, q, i : i + 1, group(lg)] if i < 4 else rows_ref[p * Q + q]
                        term = scale * value
                        acc[p] = term if acc[p] is None else acc[p] + term
                sums.append(acc)
            got.append(sums)
        local, other = got
        for p in range(Q):
            mains = [other[i][p] for i in range(4)]
            turned = fill_z(p, at_lg, mains, other[4][p], s.pick("tm", lg), s.pick("um", lg), s.zh, s.zl)
            for pair in range(2):
                high, low = halves(jnp.concatenate([local[2 * pair][p], local[2 * pair + 1][p]], axis=0))
                s.zh[p, 96 + pair * FB : 96 + (pair + 1) * FB, at_lg] = high
                s.zl[p, 96 + pair * FB : 96 + (pair + 1) * FB, at_lg] = low
            finish_z(p, at_lg, turned, local[4][p], s.zh, s.zl)
        acc = apply_star(own_star(r.star, lg), s.pick("moved", lg), group(0))
        for p in range(Q):
            out[lg][p] = base[lg][p] + acc[p]
    width = len(groups) * LANES
    for p in range(Q):
        lifted = mm(r.wl[...], s.zh[p, :, 0:width])
        rest = mm(r.wl[0:32], s.zl[p, :, 0:width])
        total = lifted[0:B] + lifted[32 : 32 + B] + rest[0:B]
        for n, lg in enumerate(groups):
            out[lg][p] = out[lg][p] - total[:, n * LANES : (n + 1) * LANES]


def build_remote(stat_ref, rhot_ref, rm_ref, ru_ref):
    index = lax.broadcasted_iota(jnp.int32, (LANES, LANES), 0).astype(F32)
    spot, side, turn, face = (stat_ref[41, r : r + 1] for r in range(1, 5))
    segment = (lax.broadcasted_iota(jnp.int32, (1, LANES), 1) // NS * NS).astype(F32)
    spot = spot + segment
    for j in range(4):
        pick = jnp.where(side == float(j), spot, -1.0)
        rhot_ref[j * LANES : (j + 1) * LANES] = jnp.where(index == pick, 1.0, 0.0).astype(BF16)
    keep_masks(lambda i, t: (face == float(i)) & (turn == float(t)), rm_ref, ru_ref)


def project_remote(field_ref, lanes, wb_ref, table_ref):
    weights = wb_ref[3 * B - 8 :]
    for q in range(Q):
        got = mm(weights, stacked(field_ref[q, :, lanes]))
        for j in range(4):
            high, low = halves(got[8 + FB * j : 8 + FB * (j + 1)])
            table_ref[q * FB : (q + 1) * FB, j * LANES : (j + 1) * LANES] = high
            table_ref[(Q + q) * FB : (Q + q + 1) * FB, j * LANES : (j + 1) * LANES] = low


def remote_part(table_ref, stat_ref, rhot_ref, rm_ref, ru_ref, wl_ref, zh_ref, zl_ref):
    rows = Q * FB
    got = mm(table_ref[...], rhot_ref[...])
    across = got[0:rows] + got[rows : 2 * rows]
    acc = [None] * Q
    for q in range(Q):
        field = across[q * FB : (q + 1) * FB]
        for p in range(Q):
            term = stat_flux(stat_ref, p, q) * field
            acc[p] = term if acc[p] is None else acc[p] + term
    nothing = jnp.zeros((8, LANES), F32)
    for p in range(Q):
        turned = fill_z(p, group(0), [acc[p][0:8]] * 4, acc[p][8:16], rm_ref, ru_ref, zh_ref, zl_ref)
        finish_z(p, group(0), turned, nothing, zh_ref, zl_ref)
    out = []
    for p in range(Q):
        lifted = mm(wl_ref[...], zh_ref[p])
        rest = mm(wl_ref[0:32], zl_ref[p])
        out.append(lifted[0:B] + lifted[32 : 32 + B] + rest[0:B])
    return out


def place_of(nbr_ref, columns):
    here = jnp.broadcast_to(nbr_ref[0:1, LANES : 2 * LANES] >> 8, (8, LANES))
    return (here // columns & 1) == 0, (here & 1) == 0


def pack(current_ref, other, stat_ref, msg_refs, even):
    blocks = []
    for p in range(Q):
        for r in range(3):
            blocks.append(current_ref[p, 8 * r : 8 * r + 8, 0:LANES])
    for p in range(Q):
        value = other(p)
        for r in range(3):
            blocks.append(value[8 * r : 8 * r + 8])
    if stat_ref is not None:
        blocks += [stat_ref[n] for n in range(STATIC)]
    while len(blocks) % 4:
        blocks.append(jnp.zeros((8, LANES), F32))
    for g in range(len(blocks) // 4):
        value = transpose_quarters(blocks[4 * g : 4 * g + 4])
        msg_refs[0][g] = jnp.where(even[0], value[1], value[0])
        msg_refs[1][g] = jnp.where(even[0], value[0], value[1])
        msg_refs[2][g] = jnp.where(even[1], value[2], value[3])
        msg_refs[3][g] = jnp.where(even[1], value[3], value[2])


def unpack(msg_refs, first, last, store, even):
    for g in range(first // 4, -(-last // 4)):
        one, two, three, last_one = (msg_refs[k][g] for k in range(4))
        four = [
            jnp.where(even[0], two, one),
            jnp.where(even[0], one, two),
            jnp.where(even[1], three, last_one),
            jnp.where(even[1], last_one, three),
        ]
        for m, value in enumerate(transpose_quarters(four)):
            if first <= 4 * g + m < last:
                store(4 * g + m - first, value)


def even_half(s, r, fine, dofs_ref, o, stat_ref):
    stars = [own_star(r.star, lg) for lg in range(2)]
    predict(dofs_ref, stars, r.wt, s.term, s.moved, [(s.cur, FIRST), (o.curo, SECOND)])
    for p in range(Q):
        o.curb[p] = s.cur[p, :, 0:LANES]
        o.base[p] = dofs_ref[p, :, LANES : 2 * LANES]
    spread_and_project(s.cur, r.wb, s)
    change_of([dofs_ref.at[:, :, 0:LANES]], [o.part0], r, s, [0])
    lead = fine[:, 0:LANES] > 0.5
    pack(
        s.cur,
        lambda p: jnp.where(lead, o.part0[p], o.curo[p, :, 0:LANES]),
        stat_ref,
        [o[key] for key in SENT],
        r.even,
    )


def rest_half(s, r, o):
    change_of([None, r.base], [None, o.part1], r, s, [1])
    project_remote(r.curb, pl.ds(0, LANES), r.wb, o.rtable2)


def odd_half(s, r, fine, ghost_ref, outs):
    def keep_table(n, value):
        s.gfield[n // 3, 8 * (n % 3) : 8 * (n % 3) + 8, :] = value

    def keep_other(n, value):
        s.dofs[n // 3, 8 * (n % 3) : 8 * (n % 3) + 8, 2 * LANES :] = value

    recv_refs = [r[key] for key in GOT]
    for p in range(Q):
        s.rzh[p, 96:128] = jnp.zeros((32, LANES), BF16)
        s.rzl[p, 96:128] = jnp.zeros((32, LANES), BF16)
    unpack(recv_refs, 0, 27, keep_table, r.even)
    unpack(recv_refs, 27, 54, keep_other, r.even)
    project_remote(s.gfield, pl.ds(0, LANES), r.wb, s.rtable)
    mine = remote_part(s.rtable, r.stat, r.rhot, r.rm, r.ru, r.wl, s.rzh, s.rzl)
    for p in range(Q):
        s.dofs[p, :, 0:LANES] = r.part0[p] - mine[p]
        s.dofs[p, :, LANES : 2 * LANES] = r.part1[p]
    theirs = remote_part(r.rtable2, ghost_ref, s.rhot2, s.rm2, s.ru2, r.wl, s.rzh, s.rzl)
    ghost_fine = ghost_ref[41, 5:6] > 0.5
    for p in range(Q):
        value = s.dofs[p, :, 2 * LANES :]
        s.gfield[p] = value
        s.dofs[p, :, 2 * LANES :] = value - theirs[p]
    stars = [own_star(r.star, 0), own_star(r.star, 1), stat_star(ghost_ref)]
    predict(s.dofs, stars, r.wt, s.term, s.moved, [(s.cur, FIRST)])
    for p in range(Q):
        s.cur[p, :, 0:256] = jnp.where(fine > 0.5, s.cur[p, :, 0:256], r.curo[p])
        s.gfield[p] = jnp.where(ghost_fine, s.cur[p, :, 256:384], s.gfield[p])
    project_remote(s.gfield, pl.ds(0, LANES), r.wb, s.rtable)
    mine = remote_part(s.rtable, r.stat, r.rhot, r.rm, r.ru, r.wl, s.rzh, s.rzl)
    for p in range(Q):
        s.dofs[p, :, 0:LANES] = s.dofs[p, :, 0:LANES] - mine[p]
    spread_and_project(s.cur, r.wb, s)
    halves_of = [s.dofs.at[:, :, group(lg)] for lg in range(2)]
    change_of(halves_of, outs, r, s, [0, 1])


FIELD = ((Q, B, LANES), F32)
SPREAD = dict(
    moved0=((Q, 3 * B, LANES), F32),
    face0=((4, Q, FB, LANES), F32),
)
KEPT = dict(
    moved1=((Q, 3 * B, LANES), F32),
    face1=((4, Q, FB, LANES), F32),
    table=((2 * Q * FB, 1024), BF16),
)
CHANGE = dict(
    across=((4, Q * FB, LANES), F32),
    zh=((Q, KZ, 256), BF16),
    zl=((Q, KZ, 256), BF16),
)
PREDICT = dict(
    dofs=((Q, B, 384), F32),
    cur=((Q, B, 384), F32),
    term=((Q, B, 384), F32),
    moved=((Q, 3 * B, 384), F32),
)
REMOTE = dict(
    gfield=FIELD,
    rtable=((2 * Q * FB, 512), BF16),
    rzh=((Q, KZ, LANES), BF16),
    rzl=((Q, KZ, LANES), BF16),
)
EVEN = dict(part0=FIELD, base=FIELD, curb=FIELD, curo=((Q, B, 256), F32), **KEPT)
GHOST_MASKS = dict(rhot2=((512, LANES), BF16), rm2=((6, FB, LANES), BF16), ru2=((3, 8, LANES), F32))
STAT = ((STATIC, 8, LANES), F32)
LOADED = ("star", "fluxl", "fluxn", "nbr", "kind", "cluster")
SMALL = ("time", "volume", "project", "rotate", "lift")


def masks(lg):
    shapes = dict(
        hot=((1024, 512), BF16), tm=((6, FB, LANES), BF16), um=((3, 8, LANES), F32),
        fpl=((Q * Q, 8, LANES), F32), fpn=((Q * Q, 8, LANES), F32),
    )
    return {key + str(lg): value for key, value in shapes.items()}


def messages(blocks):
    return {key: ((blocks // 4, 8, LANES), F32) for key in SENT}


def call(kernel, name, ins, outs, scratch, inputs, columns, hbm=False, flops=0):
    def body(*refs):
        n, m = len(ins), len(outs)
        r = Bag(zip(ins, refs[:n]))
        o = Bag(zip(outs, refs[n : n + m]))
        s = Bag(zip(scratch, refs[n + m : n + m + len(scratch)]))
        if hbm:
            sems = refs[-1]
            copies = {}
            for k, key in enumerate((*SMALL, "nbr", "kind", "cluster", "dofs", "star", "fluxn", "fluxl")):
                to = o[key] if key in LOADED else s[key + "_in"]
                copies[key] = pltpu.make_async_copy(r[key], to, sems.at[k])
                copies[key].start()
            r = Bag({key: o[key] if key in LOADED else s[key + "_in"] for key in ins})
            kernel(r, o, s, lambda *keys: [copies[key].wait() for key in keys], columns)
        else:
            r.even = place_of(r.nbr, columns)
            kernel(r, o, s)

    shapes = [pltpu.VMEM(*scratch[key]) for key in scratch]
    if hbm:
        shapes.append(pltpu.SemaphoreType.DMA((len(ins),)))
    space = pltpu.HBM if hbm else pltpu.VMEM
    got = pl.pallas_call(
        body,
        out_shape=[jax.ShapeDtypeStruct(*outs[key]) for key in outs],
        in_specs=[pl.BlockSpec(memory_space=space)] * len(ins),
        out_specs=[pl.BlockSpec(memory_space=pltpu.VMEM)] * len(outs),
        scratch_shapes=shapes,
        compiler_params=pltpu.CompilerParams(vmem_limit_bytes=24 << 20),
        cost_estimate=pl.CostEstimate(flops=flops, bytes_accessed=1 << 20, transcendentals=0),
        name=name,
    )(*(pltpu.with_memory_space_constraint(inputs[key], space) if hbm else inputs[key] for key in ins))
    return dict(zip(outs, got))


def fine_of(cluster_ref):
    return (cluster_ref[...] == 0).astype(F32)


def first_kernel(r, o, s, wait, columns):
    wait("time")
    prepare_predictor(r.time, o.wt, s.ptmp)
    wait("volume", "project", "rotate", "lift")
    prepare(r.volume, r.project, r.rotate, r.lift, o.wb, o.wl, s.ptmp, s.pturn, s.pbig)
    wait("nbr", "kind", "cluster")
    build_onehot(r.nbr, r.kind, o, [0])
    wait("dofs")
    for p in range(Q):
        s.dofs[p, 0:20, 0:256] = r.dofs[p]
        s.dofs[p, 20:B, 0:256] = jnp.zeros((B - 20, 256), F32)
    wait("star", "fluxn", "fluxl")
    keep_rows(r.fluxl, 0, o.fpl0)
    keep_rows(r.fluxn, 0, o.fpn0)
    describe(r.nbr, r.kind, r.cluster, r.star, r.fluxn, o.stat)
    r = Bag(r, wt=o.wt, wb=o.wb, wl=o.wl, even=place_of(r.nbr, columns))
    even_half(s | o, r, fine_of(r.cluster), s.dofs, o, o.stat)


def first_rest(r, o, s):
    build_onehot(r.nbr, r.kind, o, [1])
    keep_rows(r.fluxl, 1, o.fpl1)
    keep_rows(r.fluxn, 1, o.fpn1)
    build_remote(r.stat, o.rhot, o.rm, o.ru)
    rest_half(r | o | s, r, o)


def middle_kernel(r, o, s):
    def keep(n, value):
        o.ghost[n] = value

    unpack([r[key] for key in GOT], 54, 54 + STATIC, keep, r.even)
    build_remote(o.ghost, o.rhot2, o.rm2, o.ru2)
    fine = fine_of(r.cluster)
    s = r | s | o
    odd_half(s, r, fine, o.ghost, [s.next.at[:, :, group(lg)] for lg in range(2)])
    even_half(s, r, fine, s.next, o, None)


def second_rest(r, o, s):
    rest_half(r | o | s, r, o)


def last_kernel(r, o, s):
    s = r | s
    odd_half(s, r, fine_of(r.cluster), r.ghost, [s.next.at[:, :, group(lg)] for lg in range(2)])
    for p in range(Q):
        o.out[p] = s.next[p, 0:20, :]


def trade(got):
    out = {}
    for m, (axis, start) in enumerate((("px", 0), ("px", 1), ("py", 1), ("py", 0))):
        count = lax.axis_size(axis)
        pairs = []
        for low in range(start, count - 1, 2):
            pairs += [(low, low + 1), (low + 1, low)]
        out[GOT[m]] = lax.ppermute(got[SENT[m]], axis, pairs)
    return out


def per_device(dofs, star, flux_local, flux_neigh, time_stiff, volume_stiff, face_project, face_rotate, face_lift, cluster, neighbors, face_kind):
    columns = lax.axis_size("py")
    inputs = dict(
        dofs=dofs, star=star.transpose(1, 2, 0, 3), fluxl=flux_local.transpose(1, 2, 0, 3),
        fluxn=flux_neigh.transpose(1, 2, 0, 3), time=time_stiff, volume=volume_stiff,
        project=face_project.transpose(1, 0, 2), rotate=face_rotate.transpose(1, 0, 2), lift=face_lift.transpose(2, 0, 1),
        cluster=cluster.reshape(1, 256), nbr=neighbors, kind=face_kind,
    )
    first = {
        **{key: (inputs[key].shape, inputs[key].dtype) for key in LOADED},
        "wt": ((80, 80), BF16),
        "wb": ((144, 80), BF16),
        "wl": ((64, KZ), BF16),
        "stat": STAT,
        **masks(0),
        **EVEN,
        **messages(96),
    }
    scratch = {
        **PREDICT, **SPREAD, **CHANGE, "ptmp": ((144, LANES), F32), "pturn": ((LANES, LANES), F32), "pbig": ((256, LANES), F32),
        **{key + "_in": (inputs[key].shape, inputs[key].dtype) for key in (*SMALL, "dofs")},
    }
    weights = ["star", "fluxl", "fluxn", "wb", "wl", "nbr"]
    rest = {"part1": FIELD, "rtable2": ((2 * Q * FB, 512), BF16)}
    state = ["part0", "part1", "rtable2", "curo", *GOT]
    odd = weights + ["wt", "cluster", "stat", *masks(0), *masks(1), "rhot", "rm", "ru"] + state
    inputs |= call(first_kernel, "first", list(inputs), first, scratch, inputs, columns, hbm=True)
    inputs |= trade(inputs)
    inputs |= call(
        first_rest, "first_rest", weights + ["kind", "stat", "base", "curb", *KEPT],
        {**rest, **masks(1), "rhot": ((512, LANES), BF16), "rm": ((6, FB, LANES), BF16), "ru": ((3, 8, LANES), F32)},
        CHANGE, inputs, columns, flops=10**9,
    )
    both = {**PREDICT, **SPREAD, **CHANGE, **REMOTE, "next": ((Q, B, 256), F32)}
    inputs |= call(
        middle_kernel, "middle", odd, {"ghost": STAT, **GHOST_MASKS, **EVEN, **messages(56)}, both, inputs, columns,
    )
    inputs |= trade(inputs)
    inputs |= call(
        second_rest, "second_rest", weights + ["base", "curb", *masks(1), *KEPT], rest, CHANGE, inputs, columns,
        flops=10**9,
    )
    got = call(
        last_kernel, "last", odd + ["ghost", *GHOST_MASKS], {"out": ((Q, 20, 256), F32)}, {**both, **KEPT}, inputs, columns,
    )
    return got["out"]


def solution(mesh):
    cells = ("px", "py")
    placed = (
        P(None, None, cells),
        P(None, None, None, cells),
        P(None, None, None, cells),
        P(None, None, None, cells),
        P(),
        P(),
        P(),
        P(),
        P(),
        P(cells),
        P(None, cells),
        P(None, cells),
    )
    return jax.shard_map(
        per_device,
        mesh=mesh,
        in_specs=placed,
        out_specs=P(None, None, cells),
        check_vma=False,
    )
```

time: 69 us -> 46.2 us (0.67)
  starting transfers between devices: 28.1 us -> 18.5 us
  waiting for transfers between devices: 7.12 us -> 0.76 us
  local copies, waits for them, and re-layouts: 4.56 us -> 0 us
  Pallas kernels: 28.6 us -> 26.1 us
    ppermute x8, starting transfers between devices: 28.1 us -> 18.5 us  [trade(): out[GOT[m]] = lax.ppermute(got[SENT[m]], axis, pairs)]
    ppermute x8, waiting for transfers between devices: 7.12 us -> 0.76 us  [trade(): out[GOT[m]] = lax.ppermute(got[SENT[m]], axis, pairs)]
    unnamed x26 -> x0, local copies, waits for them, and re-layouts: 4.56 us -> none
    pallas_call x3 -> x5, Pallas kernels: 28.6 us -> 26.1 us  [call(): pl.pallas_call(body, out_shape=[jax.ShapeDtypeStruct(*outs[key]) for key...]
  transfers between devices with their start and end apart: 8 -> 8, of which waited for: 2 -> 2; matrix products, arithmetic and copies ran while one was open for 0% -> 0% of each run, Pallas kernels for 0% -> 7%
where the time goes in v1:
time: 46.2 us; the launch traced here: 45.5 us
  Pallas kernels  26.1 us (56%)
  starting transfers between devices  18.5 us (40%)
  waiting for transfers between devices  0.76 us (2%)
    pallas_call x5, Pallas kernels, call(): pl.pallas_call(body, out_shape=[jax.ShapeDtypeStruct(*outs[key]) for key...  26.1 us
    ppermute x8, starting transfers between devices, trade(): out[GOT[m]] = lax.ppermute(got[SENT[m]], axis, pairs)  18.5 us
  transfers between devices with their start and end apart: 8, of which 2 were waited for; matrix products, arithmetic and copies ran while one was open for 0% of the time, Pallas kernels for 7%

profile of v1, /device:TPU:129, one launch (start us, length us, event | category | flops | bytes accessed | tf_op | source)
XLA Modules:
  0.0 45.5 jit_solution(11312102226228993665)
XLA Ops:
  0.0 5.5 %first.1 = (f32[9,9,3,256]{3,2,1,0:T(4,128)S(1)}, f32[9,9,4,256]{3,2,1,0:T(4,128)S(1)}, f32[9,9,4,256]{3,2,1,0:T(4,128)S(1)}, s32[4,256]{1,0:T(4,128)S(1)}, s32[...) custom-call(f32[9,20,256]{2,1,0:T(8,128)} %refs_0_.1, ...), custom_call_target="tpu_custom_call" | custom-call | bytes 1048576 | tf_op jit(solution)/shard_map/first/pallas_call | solution.py:551
  5.5 1.4 %collective-permute-start = (f32[24,8,128]{2,1,0:T(8,128)S(1)}, f32[24,8,128]{2,1,0:T(8,128)S(1)}, u32[]{:S(2)}, u32[]{:S(2)}) collective-permute-start(f32[24,8,128]{2,1,0:T(8,128)S(1)} %get-tuple-element.90), channel_id=1, source_target_pairs={{0,8},{8,0},{16,24},{24,16},{32,40},{40,32},{48,56},{56,48},{64,72... | collective-permute-start | bytes 294920 | tf_op jit(solution)/shard_map/ppermute | solution.py:625
  6.8 3.3 %collective-permute-start.1 = (f32[24,8,128]{2,1,0:T(8,128)S(1)}, f32[24,8,128]{2,1,0:T(8,128)S(1)}, u32[]{:S(2)}, u32[]{:S(2)}) collective-permute-start(f32[24,8,128]{2,1,0:T(8,128)S(1)} %get-tuple-element.91), channel_id=1, source_target_pairs={{8,16},{16,8},{24,32},{32,24},{40,48},{48,40},{56,64},{64,56},{72,... | collective-permute-start | bytes 294920 | tf_op jit(solution)/shard_map/ppermute | solution.py:625
  10.2 4.2 %collective-permute-start.2 = (f32[24,8,128]{2,1,0:T(8,128)S(1)}, f32[24,8,128]{2,1,0:T(8,128)S(1)}, u32[]{:S(2)}, u32[]{:S(2)}) collective-permute-start(f32[24,8,128]{2,1,0:T(8,128)S(1)} %get-tuple-element.92), channel_id=1, source_target_pairs={{1,2},{2,1},{3,4},{4,3},{5,6},{6,5},{9,10},{10,9},{11,12},{12,11},... | collective-permute-start | bytes 294920 | tf_op jit(solution)/shard_map/ppermute | solution.py:625
  14.4 0.3 collective-permute-start.3
  14.7 1.6 %first_rest.1 = (f32[9,24,128]{2,1,0:T(8,128)S(1)}, bf16[288,512]{1,0:T(8,128)(2,1)S(1)}, bf16[1024,512]{1,0:T(8,128)(2,1)S(1)}, bf16[6,16,128]{2,1,0:T(8,128)(2...) custom-call(f32[9,9,3,256]{3,2,1,0:T(4,128)S(1)} %get-tuple-element., ...), custom_call_target="tpu_custom_call" | custom-call | flops 1000000000 | bytes 1048576 | tf_op jit(solution)/shard_map/first_rest/pallas_call | solution.py:551
  16.4 0.0 collective-permute-done.refs_26_
  16.4 0.0 collective-permute-done.1.refs_27_
  16.4 0.6 %collective-permute-done.2.refs_28_ = f32[24,8,128]{2,1,0:T(8,128)S(1)} collective-permute-done((f32[24,8,128]{2,1,0:T(8,128)S(1)}, f32[24,8,128]{2,1,0:T(8,128)S(1)}, u32[]{:S(2)}, u32[]{:S(2)}) %collective-permute-start.2) | collective-permute-done | bytes 98336 | tf_op jit(solution)/shard_map/ppermute | solution.py:625
  17.0 0.0 collective-permute-done.3.refs_29_
  17.0 10.2 %middle.1 = (f32[42,8,128]{2,1,0:T(8,128)S(1)}, bf16[512,128]{1,0:T(8,128)(2,1)S(1)}, bf16[6,16,128]{2,1,0:T(8,128)(2,1)S(1)}, f32[3,8,128]{2,1,0:T(8,128)S(1)},...) custom-call(f32[9,9,3,256]{3,2,1,0:T(4,128)S(1)} %get-tuple-element., ...), custom_call_target="tpu_custom_call" | custom-call | bytes 1048576 | tf_op jit(solution)/shard_map/middle/pallas_call | solution.py:551
  27.2 0.6 %collective-permute-start.4 = (f32[14,8,128]{2,1,0:T(8,128)S(1)}, f32[14,8,128]{2,1,0:T(8,128)S(1)}, u32[]{:S(2)}, u32[]{:S(2)}) collective-permute-start(f32[14,8,128]{2,1,0:T(8,128)S(1)} %get-tuple-element.103), channel_id=1, source_target_pairs={{0,8},{8,0},{16,24},{24,16},{32,40},{40,32},{48,56},{56,48},{64,72... | collective-permute-start | bytes 172040 | tf_op jit(solution)/shard_map/ppermute | solution.py:625
  27.8 4.4 %collective-permute-start.5 = (f32[14,8,128]{2,1,0:T(8,128)S(1)}, f32[14,8,128]{2,1,0:T(8,128)S(1)}, u32[]{:S(2)}, u32[]{:S(2)}) collective-permute-start(f32[14,8,128]{2,1,0:T(8,128)S(1)} %get-tuple-element.104), channel_id=1, source_target_pairs={{8,16},{16,8},{24,32},{32,24},{40,48},{48,40},{56,64},{64,56},{72,... | collective-permute-start | bytes 172040 | tf_op jit(solution)/shard_map/ppermute | solution.py:625
  32.3 3.9 %collective-permute-start.6 = (f32[14,8,128]{2,1,0:T(8,128)S(1)}, f32[14,8,128]{2,1,0:T(8,128)S(1)}, u32[]{:S(2)}, u32[]{:S(2)}) collective-permute-start(f32[14,8,128]{2,1,0:T(8,128)S(1)} %get-tuple-element.105), channel_id=1, source_target_pairs={{1,2},{2,1},{3,4},{4,3},{5,6},{6,5},{9,10},{10,9},{11,12},{12,11},... | collective-permute-start | bytes 172040 | tf_op jit(solution)/shard_map/ppermute | solution.py:625
  36.2 0.3 collective-permute-start.7
  36.5 1.4 %second_rest.1 = (f32[9,24,128]{2,1,0:T(8,128)S(1)}, bf16[288,512]{1,0:T(8,128)(2,1)S(1)}) custom-call(f32[9,9,3,256]{3,2,1,0:T(4,128)S(1)} %get-tuple-element.58.refs_0_, f32[9,9,4,256]{3,2,1,0:T(4,128)S(1)} %get-tuple-element.59.refs_1_, f32[9,9,4,256]{3,2,1,0:T(4,128)S(1)} %get-tuple-element.60.refs_2_, bf16[144,80]{1,0:T(8,128)(2,1)S(1)} %get-tuple-element.61.refs_3_, ...), custom_call_target="tpu_custom_call" | custom-call | flops 1000000000 | bytes 1048576 | tf_op jit(solution)/shard_map/second_rest/pallas_call | solution.py:551
  37.9 0.0 collective-permute-done.4.refs_26_
  37.9 0.0 collective-permute-done.5.refs_27_
  37.9 0.1 collective-permute-done.6.refs_28_
  38.0 0.0 collective-permute-done.7.refs_29_
  38.0 7.5 %last.1 = f32[9,20,256]{2,1,0:T(8,128)} custom-call(f32[9,9,3,256]{3,2,1,0:T(4,128)S(1)} %get-tuple-element.58.refs_0_, f32[9,9,4,256]{3,2,1,0:T(4,128)S(1)} %get-tuple-element.59.refs_1_, f32[9,9,4,256]{3,2,1,0:T(4,128)S(1)} %get-tuple-element.60.refs_2_, bf16[144,80]{1,0:T(8,128)(2,1)S(1)} %get-tuple-element.61.refs_3_, ...), custom_call_target="tpu_custom_call" | custom-call | bytes 1048576 | tf_op jit(solution)/shard_map/last/pallas_call | solution.py:551
Async XLA Ops:
  5.5 10.9 %collective-permute-start = (f32[24,8,128]{2,1,0:T(8,128)S(1)}, f32[24,8,128]{2,1,0:T(8,128)S(1)}, u32[]{:S(2)}, u32[]{:S(2)}) collective-permute-start(f32[24,8,128]{2,1,0:T(8,128)S(1)} %get-tuple-element.90), channel_id=1, source_target_pairs={{0,8},{8,0},{16,24},{24,16},{32,40},{40,32},{48,56},{56,48},{64,72... | collective-permute-start | bytes 294920 | tf_op jit(solution)/shard_map/ppermute | solution.py:625
  6.8 9.5 %collective-permute-start.1 = (f32[24,8,128]{2,1,0:T(8,128)S(1)}, f32[24,8,128]{2,1,0:T(8,128)S(1)}, u32[]{:S(2)}, u32[]{:S(2)}) collective-permute-start(f32[24,8,128]{2,1,0:T(8,128)S(1)} %get-tuple-element.91), channel_id=1, source_target_pairs={{8,16},{16,8},{24,32},{32,24},{40,48},{48,40},{56,64},{64,56},{72,... | collective-permute-start | bytes 294920 | tf_op jit(solution)/shard_map/ppermute | solution.py:625
  10.2 6.8 %collective-permute-start.2 = (f32[24,8,128]{2,1,0:T(8,128)S(1)}, f32[24,8,128]{2,1,0:T(8,128)S(1)}, u32[]{:S(2)}, u32[]{:S(2)}) collective-permute-start(f32[24,8,128]{2,1,0:T(8,128)S(1)} %get-tuple-element.92), channel_id=1, source_target_pairs={{1,2},{2,1},{3,4},{4,3},{5,6},{6,5},{9,10},{10,9},{11,12},{12,11},... | collective-permute-start | bytes 294920 | tf_op jit(solution)/shard_map/ppermute | solution.py:625
  14.4 2.6 %collective-permute-start.3 = (f32[24,8,128]{2,1,0:T(8,128)S(1)}, f32[24,8,128]{2,1,0:T(8,128)S(1)}, u32[]{:S(2)}, u32[]{:S(2)}) collective-permute-start(f32[24,8,128]{2,1,0:T(8,128)S(1)} %get-tuple-element.93), channel_id=1, source_target_pairs={{0,1},{1,0},{2,3},{3,2},{4,5},{5,4},{6,7},{7,6},{8,9},{9,8},{10,11... | collective-permute-start | bytes 294920 | tf_op jit(solution)/shard_map/ppermute | solution.py:625
  27.2 10.7 %collective-permute-start.4 = (f32[14,8,128]{2,1,0:T(8,128)S(1)}, f32[14,8,128]{2,1,0:T(8,128)S(1)}, u32[]{:S(2)}, u32[]{:S(2)}) collective-permute-start(f32[14,8,128]{2,1,0:T(8,128)S(1)} %get-tuple-element.103), channel_id=1, source_target_pairs={{0,8},{8,0},{16,24},{24,16},{32,40},{40,32},{48,56},{56,48},{64,72... | collective-permute-start | bytes 172040 | tf_op jit(solution)/shard_map/ppermute | solution.py:625
  27.8 10.1 %collective-permute-start.5 = (f32[14,8,128]{2,1,0:T(8,128)S(1)}, f32[14,8,128]{2,1,0:T(8,128)S(1)}, u32[]{:S(2)}, u32[]{:S(2)}) collective-permute-start(f32[14,8,128]{2,1,0:T(8,128)S(1)} %get-tuple-element.104), channel_id=1, source_target_pairs={{8,16},{16,8},{24,32},{32,24},{40,48},{48,40},{56,64},{64,56},{72,... | collective-permute-start | bytes 172040 | tf_op jit(solution)/shard_map/ppermute | solution.py:625
  32.3 5.8 %collective-permute-start.6 = (f32[14,8,128]{2,1,0:T(8,128)S(1)}, f32[14,8,128]{2,1,0:T(8,128)S(1)}, u32[]{:S(2)}, u32[]{:S(2)}) collective-permute-start(f32[14,8,128]{2,1,0:T(8,128)S(1)} %get-tuple-element.105), channel_id=1, source_target_pairs={{1,2},{2,1},{3,4},{4,3},{5,6},{6,5},{9,10},{10,9},{11,12},{12,11},... | collective-permute-start | bytes 172040 | tf_op jit(solution)/shard_map/ppermute | solution.py:625
  36.2 1.9 %collective-permute-start.7 = (f32[14,8,128]{2,1,0:T(8,128)S(1)}, f32[14,8,128]{2,1,0:T(8,128)S(1)}, u32[]{:S(2)}, u32[]{:S(2)}) collective-permute-start(f32[14,8,128]{2,1,0:T(8,128)S(1)} %get-tuple-element.106), channel_id=1, source_target_pairs={{0,1},{1,0},{2,3},{3,2},{4,5},{5,4},{6,7},{7,6},{8,9},{9,8},{10,11... | collective-permute-start | bytes 172040 | tf_op jit(solution)/shard_map/ppermute | solution.py:625

commit v2 on v1

--- a/solution.py
+++ b/solution.py
@@ -233,21 +233,31 @@
             rows_ref[p * Q + q, 4:8] = tile
 
 
-def fill_z(p, lanes, mains, last, pair_ref, last_ref, zh_ref, zl_ref):
+def fill_z(lanes, mains, last, pair_ref, last_ref, zh_ref, zl_ref):
     for pair in range(2):
         high, low = halves(jnp.concatenate(mains[2 * pair : 2 * pair + 2], axis=0))
         for t in range(3):
             at = pl.ds((pair * 3 + t) * FB, FB)
-            zh_ref[p, at, lanes] = high * pair_ref[pair * 3 + t]
-            zl_ref[p, at, lanes] = low * pair_ref[pair * 3 + t]
+            zh_ref[at, lanes] = high * pair_ref[pair * 3 + t]
+            zl_ref[at, lanes] = low * pair_ref[pair * 3 + t]
     return [last * last_ref[t] for t in range(3)]
 
 
-def finish_z(p, lanes, turned, local, zh_ref, zl_ref):
+def finish_z(lanes, turned, local, zh_ref, zl_ref):
     for n, two in enumerate(((turned[0], turned[1]), (turned[2], local))):
         high, low = halves(jnp.concatenate(two, axis=0))
-        zh_ref[p, 128 + n * FB : 128 + (n + 1) * FB, lanes] = high
-        zl_ref[p, 128 + n * FB : 128 + (n + 1) * FB, lanes] = low
+        zh_ref[128 + n * FB : 128 + (n + 1) * FB, lanes] = high
+        zl_ref[128 + n * FB : 128 + (n + 1) * FB, lanes] = low
+
+
+def lift(wl_ref, zh_ref, zl_ref, width, store):
+    for start in range(0, Q * width, 2 * LANES):
+        stop = min(start + 2 * LANES, Q * width)
+        lifted = mm(wl_ref[...], zh_ref[:, start:stop])
+        rest = mm(wl_ref[0:32], zl_ref[:, start:stop])
+        total = lifted[0:B] + lifted[32 : 32 + B] + rest[0:B]
+        for p in range(start // width, stop // width):
+            store(p, total[:, p * width - start : (p + 1) * width - start])
 
 
 def build_onehot(nbr_ref, kind_ref, s, groups):
@@ -286,7 +296,6 @@
 def change_of(base, out, r, s, groups):
     rows = Q * FB
     for lg in groups:
-        at_lg = group(groups.index(lg))
         for pair in range(2):
             cols = pl.ds(2 * pair * LANES, 2 * LANES)
             got = mm(s.table[...], s.pick("hot", lg)[:, cols])
@@ -317,22 +326,22 @@
         local, other = got
         for p in range(Q):
             mains = [other[i][p] for i in range(4)]
-            turned = fill_z(p, at_lg, mains, other[4][p], s.pick("tm", lg), s.pick("um", lg), s.zh, s.zl)
+            at_lg = group(p * len(groups) + groups.index(lg))
+            turned = fill_z(at_lg, mains, other[4][p], s.pick("tm", lg), s.pick("um", lg), s.zh, s.zl)
             for pair in range(2):
                 high, low = halves(jnp.concatenate([local[2 * pair][p], local[2 * pair + 1][p]], axis=0))
-                s.zh[p, 96 + pair * FB : 96 + (pair + 1) * FB, at_lg] = high
-                s.zl[p, 96 + pair * FB : 96 + (pair + 1) * FB, at_lg] = low
-            finish_z(p, at_lg, turned, local[4][p], s.zh, s.zl)
+                s.zh[96 + pair * FB : 96 + (pair + 1) * FB, at_lg] = high
+                s.zl[96 + pair * FB : 96 + (pair + 1) * FB, at_lg] = low
+            finish_z(at_lg, turned, local[4][p], s.zh, s.zl)
         acc = apply_star(own_star(r.star, lg), s.pick("moved", lg), group(0))
         for p in range(Q):
             out[lg][p] = base[lg][p] + acc[p]
-    width = len(groups) * LANES
-    for p in range(Q):
-        lifted = mm(r.wl[...], s.zh[p, :, 0:width])
-        rest = mm(r.wl[0:32], s.zl[p, :, 0:width])
-        total = lifted[0:B] + lifted[32 : 32 + B] + rest[0:B]
+
+    def store(p, total):
         for n, lg in enumerate(groups):
             out[lg][p] = out[lg][p] - total[:, n * LANES : (n + 1) * LANES]
+
+    lift(r.wl, s.zh, s.zl, len(groups) * LANES, store)
 
 
 def build_remote(stat_ref, rhot_ref, rm_ref, ru_ref):
@@ -346,17 +355,21 @@
     keep_masks(lambda i, t: (face == float(i)) & (turn == float(t)), rm_ref, ru_ref)
 
 
-def project_remote(field_ref, lanes, wb_ref, table_ref):
+def project_remote(field_ref, wb_ref, table_ref):
     weights = wb_ref[3 * B - 8 :]
-    for q in range(Q):
-        got = mm(weights, stacked(field_ref[q, :, lanes]))
-        for j in range(4):
-            high, low = halves(got[8 + FB * j : 8 + FB * (j + 1)])
-            table_ref[q * FB : (q + 1) * FB, j * LANES : (j + 1) * LANES] = high
-            table_ref[(Q + q) * FB : (Q + q + 1) * FB, j * LANES : (j + 1) * LANES] = low
-
-
-def remote_part(table_ref, stat_ref, rhot_ref, rm_ref, ru_ref, wl_ref, zh_ref, zl_ref):
+    fields = [stacked(field_ref[q]) for q in range(Q)]
+    for start in range(0, Q, 2):
+        two = fields[start : start + 2]
+        got = mm(weights, jnp.concatenate(two, axis=1))
+        for n in range(len(two)):
+            q = start + n
+            for j in range(4):
+                high, low = halves(got[8 + FB * j : 8 + FB * (j + 1), n * LANES : (n + 1) * LANES])
+                table_ref[q * FB : (q + 1) * FB, j * LANES : (j + 1) * LANES] = high
+                table_ref[(Q + q) * FB : (Q + q + 1) * FB, j * LANES : (j + 1) * LANES] = low
+
+
+def remote_z(table_ref, stat_ref, rhot_ref, rm_ref, ru_ref, s, place):
     rows = Q * FB
     got = mm(table_ref[...], rhot_ref[...])
     across = got[0:rows] + got[rows : 2 * rows]
@@ -368,14 +381,9 @@
             acc[p] = term if acc[p] is None else acc[p] + term
     nothing = jnp.zeros((8, LANES), F32)
     for p in range(Q):
-        turned = fill_z(p, group(0), [acc[p][0:8]] * 4, acc[p][8:16], rm_ref, ru_ref, zh_ref, zl_ref)
-        finish_z(p, group(0), turned, nothing, zh_ref, zl_ref)
-    out = []
-    for p in range(Q):
-        lifted = mm(wl_ref[...], zh_ref[p])
-        rest = mm(wl_ref[0:32], zl_ref[p])
-        out.append(lifted[0:B] + lifted[32 : 32 + B] + rest[0:B])
-    return out
+        lanes = group(place(p))
+        turned = fill_z(lanes, [acc[p][0:8]] * 4, acc[p][8:16], rm_ref, ru_ref, s.rzh, s.rzl)
+        finish_z(lanes, turned, nothing, s.rzh, s.rzl)
 
 
 def place_of(nbr_ref, columns):
@@ -438,7 +446,8 @@
 
 def rest_half(s, r, o):
     change_of([None, r.base], [None, o.part1], r, s, [1])
-    project_remote(r.curb, pl.ds(0, LANES), r.wb, o.rtable2)
+    project_remote(r.curb, r.wb, o.rtable2)
+    predict(o.part1, [own_star(r.star, 1)], r.wt, s.term1, s.pmoved1, [(o.ahead, FIRST)])
 
 
 def odd_half(s, r, fine, ghost_ref, outs):
@@ -446,37 +455,40 @@
         s.gfield[n // 3, 8 * (n % 3) : 8 * (n % 3) + 8, :] = value
 
     def keep_other(n, value):
-        s.dofs[n // 3, 8 * (n % 3) : 8 * (n % 3) + 8, 2 * LANES :] = value
+        s.dofs[n // 3, 8 * (n % 3) : 8 * (n % 3) + 8, LANES : 2 * LANES] = value
 
     recv_refs = [r[key] for key in GOT]
-    for p in range(Q):
-        s.rzh[p, 96:128] = jnp.zeros((32, LANES), BF16)
-        s.rzl[p, 96:128] = jnp.zeros((32, LANES), BF16)
+    s.rzh[96:128] = jnp.zeros((32, s.rzh.shape[1]), BF16)
+    s.rzl[96:128] = jnp.zeros((32, s.rzl.shape[1]), BF16)
     unpack(recv_refs, 0, 27, keep_table, r.even)
     unpack(recv_refs, 27, 54, keep_other, r.even)
-    project_remote(s.gfield, pl.ds(0, LANES), r.wb, s.rtable)
-    mine = remote_part(s.rtable, r.stat, r.rhot, r.rm, r.ru, r.wl, s.rzh, s.rzl)
-    for p in range(Q):
-        s.dofs[p, :, 0:LANES] = r.part0[p] - mine[p]
-        s.dofs[p, :, LANES : 2 * LANES] = r.part1[p]
-    theirs = remote_part(r.rtable2, ghost_ref, s.rhot2, s.rm2, s.ru2, r.wl, s.rzh, s.rzl)
+    project_remote(s.gfield, r.wb, s.rtable)
+    remote_z(s.rtable, r.stat, r.rhot, r.rm, r.ru, s, lambda p: 2 * p)
+    remote_z(r.rtable2, ghost_ref, s.rhot2, s.rm2, s.ru2, s, lambda p: 2 * p + 1)
+
+    def first_store(p, total):
+        value = s.dofs[p, :, LANES : 2 * LANES]
+        s.gfield[p] = value
+        s.dofs[p, :, LANES : 2 * LANES] = value - total[:, LANES : 2 * LANES]
+        s.dofs[p, :, 0:LANES] = r.part0[p] - total[:, 0:LANES]
+
+    lift(r.wl, s.rzh, s.rzl, 2 * LANES, first_store)
     ghost_fine = ghost_ref[41, 5:6] > 0.5
-    for p in range(Q):
-        value = s.dofs[p, :, 2 * LANES :]
-        s.gfield[p] = value
-        s.dofs[p, :, 2 * LANES :] = value - theirs[p]
-    stars = [own_star(r.star, 0), own_star(r.star, 1), stat_star(ghost_ref)]
-    predict(s.dofs, stars, r.wt, s.term, s.moved, [(s.cur, FIRST)])
-    for p in range(Q):
-        s.cur[p, :, 0:256] = jnp.where(fine > 0.5, s.cur[p, :, 0:256], r.curo[p])
-        s.gfield[p] = jnp.where(ghost_fine, s.cur[p, :, 256:384], s.gfield[p])
-    project_remote(s.gfield, pl.ds(0, LANES), r.wb, s.rtable)
-    mine = remote_part(s.rtable, r.stat, r.rhot, r.rm, r.ru, r.wl, s.rzh, s.rzl)
-    for p in range(Q):
-        s.dofs[p, :, 0:LANES] = s.dofs[p, :, 0:LANES] - mine[p]
+    stars = [own_star(r.star, 0), stat_star(ghost_ref)]
+    predict(s.dofs, stars, r.wt, s.term, s.moved, [(s.edge, FIRST)])
+    for p in range(Q):
+        s.cur[p, :, 0:LANES] = jnp.where(fine[:, 0:LANES] > 0.5, s.edge[p, :, 0:LANES], r.curo[p, :, 0:LANES])
+        s.cur[p, :, LANES:256] = jnp.where(fine[:, LANES:256] > 0.5, r.ahead[p], r.curo[p, :, LANES:256])
+        s.gfield[p] = jnp.where(ghost_fine, s.edge[p, :, LANES:256], s.gfield[p])
+    project_remote(s.gfield, r.wb, s.rtable)
     spread_and_project(s.cur, r.wb, s)
-    halves_of = [s.dofs.at[:, :, group(lg)] for lg in range(2)]
-    change_of(halves_of, outs, r, s, [0, 1])
+    remote_z(s.rtable, r.stat, r.rhot, r.rm, r.ru, s, lambda p: p)
+
+    def second_store(p, total):
+        s.dofs[p, :, 0:LANES] = s.dofs[p, :, 0:LANES] - total
+
+    lift(r.wl, s.rzh, s.rzl, LANES, second_store)
+    change_of([s.dofs.at[:, :, 0:LANES], r.part1], outs, r, s, [0, 1])
 
 
 FIELD = ((Q, B, LANES), F32)
@@ -491,20 +503,21 @@
 )
 CHANGE = dict(
     across=((4, Q * FB, LANES), F32),
-    zh=((Q, KZ, 256), BF16),
-    zl=((Q, KZ, 256), BF16),
+    zh=((KZ, Q * 256), BF16),
+    zl=((KZ, Q * 256), BF16),
 )
 PREDICT = dict(
-    dofs=((Q, B, 384), F32),
-    cur=((Q, B, 384), F32),
-    term=((Q, B, 384), F32),
-    moved=((Q, 3 * B, 384), F32),
+    dofs=((Q, B, 256), F32),
+    cur=((Q, B, 256), F32),
+    term=((Q, B, 256), F32),
+    moved=((Q, 3 * B, 256), F32),
 )
 REMOTE = dict(
     gfield=FIELD,
+    edge=((Q, B, 256), F32),
     rtable=((2 * Q * FB, 512), BF16),
-    rzh=((Q, KZ, LANES), BF16),
-    rzl=((Q, KZ, LANES), BF16),
+    rzh=((KZ, Q * 256), BF16),
+    rzl=((KZ, Q * 256), BF16),
 )
 EVEN = dict(part0=FIELD, base=FIELD, curb=FIELD, curo=((Q, B, 256), F32), **KEPT)
 GHOST_MASKS = dict(rhot2=((512, LANES), BF16), rm2=((6, FB, LANES), BF16), ru2=((3, 8, LANES), F32))
@@ -648,16 +661,17 @@
         **PREDICT, **SPREAD, **CHANGE, "ptmp": ((144, LANES), F32), "pturn": ((LANES, LANES), F32), "pbig": ((256, LANES), F32),
         **{key + "_in": (inputs[key].shape, inputs[key].dtype) for key in (*SMALL, "dofs")},
     }
-    weights = ["star", "fluxl", "fluxn", "wb", "wl", "nbr"]
-    rest = {"part1": FIELD, "rtable2": ((2 * Q * FB, 512), BF16)}
-    state = ["part0", "part1", "rtable2", "curo", *GOT]
-    odd = weights + ["wt", "cluster", "stat", *masks(0), *masks(1), "rhot", "rm", "ru"] + state
+    alone = dict(**CHANGE, term1=FIELD, pmoved1=((Q, 3 * B, LANES), F32))
+    weights = ["star", "fluxl", "fluxn", "wt", "wb", "wl", "nbr"]
+    rest = {"part1": FIELD, "ahead": FIELD, "rtable2": ((2 * Q * FB, 512), BF16)}
+    state = ["part0", "part1", "ahead", "rtable2", "curo", *GOT]
+    odd = weights + ["cluster", "stat", *masks(0), *masks(1), "rhot", "rm", "ru"] + state
     inputs |= call(first_kernel, "first", list(inputs), first, scratch, inputs, columns, hbm=True)
     inputs |= trade(inputs)
     inputs |= call(
         first_rest, "first_rest", weights + ["kind", "stat", "base", "curb", *KEPT],
         {**rest, **masks(1), "rhot": ((512, LANES), BF16), "rm": ((6, FB, LANES), BF16), "ru": ((3, 8, LANES), F32)},
-        CHANGE, inputs, columns, flops=10**9,
+        alone, inputs, columns, flops=10**9,
     )
     both = {**PREDICT, **SPREAD, **CHANGE, **REMOTE, "next": ((Q, B, 256), F32)}
     inputs |= call(
@@ -665,7 +679,7 @@
     )
     inputs |= trade(inputs)
     inputs |= call(
-        second_rest, "second_rest", weights + ["base", "curb", *masks(1), *KEPT], rest, CHANGE, inputs, columns,
+        second_rest, "second_rest", weights + ["base", "curb", *masks(1), *KEPT], rest, alone, inputs, columns,
         flops=10**9,
     )
     got = call(

time: 46.2 us -> 43.7 us (0.946)
  Pallas kernels: 26.1 us -> 24.4 us
  waiting for transfers between devices: 0.76 us -> 0.02 us
    pallas_call x5, Pallas kernels: 26.1 us -> 24.4 us  [call(): pl.pallas_call(body, out_shape=[jax.ShapeDtypeStruct(*outs[key]) for key...]
    ppermute x8, waiting for transfers between devices: 0.76 us -> 0.02 us  [trade(): out[GOT[m]] = lax.ppermute(got[SENT[m]], axis, pairs)]
  transfers between devices with their start and end apart: 8 -> 8, of which waited for: 2 -> 0; matrix products, arithmetic and copies ran while one was open for 0% -> 0% of each run, Pallas kernels for 7% -> 11%
where the time goes in v2:
time: 43.7 us; the launch traced here: 43.2 us
  Pallas kernels  24.4 us (56%)
  starting transfers between devices  18.7 us (43%)
    pallas_call x5, Pallas kernels, call(): pl.pallas_call(body, out_shape=[jax.ShapeDtypeStruct(*outs[key]) for key...  24.4 us
    ppermute x8, starting transfers between devices, trade(): out[GOT[m]] = lax.ppermute(got[SENT[m]], axis, pairs)  18.7 us
  transfers between devices with their start and end apart: 8, of which 0 were waited for; matrix products, arithmetic and copies ran while one was open for 0% of the time, Pallas kernels for 11%

profile of v2, /device:TPU:129, one launch (start us, length us, event | category | flops | bytes accessed | tf_op | source)
XLA Modules:
  0.0 43.2 jit_solution(3874825056393624784)
XLA Ops:
  0.0 5.3 %first.1 = (f32[9,9,3,256]{3,2,1,0:T(4,128)S(1)}, f32[9,9,4,256]{3,2,1,0:T(4,128)S(1)}, f32[9,9,4,256]{3,2,1,0:T(4,128)S(1)}, s32[4,256]{1,0:T(4,128)S(1)}, s32[...) custom-call(f32[9,20,256]{2,1,0:T(8,128)} %refs_0_.1, ...), custom_call_target="tpu_custom_call" | custom-call | bytes 1048576 | tf_op jit(solution)/shard_map/first/pallas_call | solution.py:564
  5.3 1.4 %collective-permute-start = (f32[24,8,128]{2,1,0:T(8,128)S(1)}, f32[24,8,128]{2,1,0:T(8,128)S(1)}, u32[]{:S(2)}, u32[]{:S(2)}) collective-permute-start(f32[24,8,128]{2,1,0:T(8,128)S(1)} %get-tuple-element.93), channel_id=1, source_target_pairs={{0,8},{8,0},{16,24},{24,16},{32,40},{40,32},{48,56},{56,48},{64,72... | collective-permute-start | bytes 294920 | tf_op jit(solution)/shard_map/ppermute | solution.py:638
  6.7 3.3 %collective-permute-start.1 = (f32[24,8,128]{2,1,0:T(8,128)S(1)}, f32[24,8,128]{2,1,0:T(8,128)S(1)}, u32[]{:S(2)}, u32[]{:S(2)}) collective-permute-start(f32[24,8,128]{2,1,0:T(8,128)S(1)} %get-tuple-element.94), channel_id=1, source_target_pairs={{8,16},{16,8},{24,32},{32,24},{40,48},{48,40},{56,64},{64,56},{72,... | collective-permute-start | bytes 294920 | tf_op jit(solution)/shard_map/ppermute | solution.py:638
  10.0 4.2 %collective-permute-start.2 = (f32[24,8,128]{2,1,0:T(8,128)S(1)}, f32[24,8,128]{2,1,0:T(8,128)S(1)}, u32[]{:S(2)}, u32[]{:S(2)}) collective-permute-start(f32[24,8,128]{2,1,0:T(8,128)S(1)} %get-tuple-element.95), channel_id=1, source_target_pairs={{1,2},{2,1},{3,4},{4,3},{5,6},{6,5},{9,10},{10,9},{11,12},{12,11},... | collective-permute-start | bytes 294920 | tf_op jit(solution)/shard_map/ppermute | solution.py:638
  14.3 0.3 collective-permute-start.3
  14.6 2.4 %first_rest.1 = (f32[9,24,128]{2,1,0:T(8,128)S(1)}, f32[9,24,128]{2,1,0:T(8,128)S(1)}, bf16[288,512]{1,0:T(8,128)(2,1)S(1)}, bf16[1024,512]{1,0:T(8,128)(2,1)S(1...) custom-call(f32[9,9,3,256]{3,2,1,0:T(4,128)S(1)} %get-tuple-element., ...), custom_call_target="tpu_custom_call" | custom-call | flops 1000000000 | bytes 1048576 | tf_op jit(solution)/shard_map/first_rest/pallas_call | solution.py:564
  17.0 0.0 collective-permute-done.refs_27_
  17.0 0.0 collective-permute-done.1.refs_28_
  17.0 0.0 collective-permute-done.2.refs_29_
  17.0 0.0 collective-permute-done.3.refs_30_
  17.0 8.5 %middle.1 = (f32[42,8,128]{2,1,0:T(8,128)S(1)}, bf16[512,128]{1,0:T(8,128)(2,1)S(1)}, bf16[6,16,128]{2,1,0:T(8,128)(2,1)S(1)}, f32[3,8,128]{2,1,0:T(8,128)S(1)},...) custom-call(f32[9,9,3,256]{3,2,1,0:T(4,128)S(1)} %get-tuple-element., ...), custom_call_target="tpu_custom_call" | custom-call | bytes 1048576 | tf_op jit(solution)/shard_map/middle/pallas_call | solution.py:564
  25.5 0.9 %collective-permute-start.4 = (f32[14,8,128]{2,1,0:T(8,128)S(1)}, f32[14,8,128]{2,1,0:T(8,128)S(1)}, u32[]{:S(2)}, u32[]{:S(2)}) collective-permute-start(f32[14,8,128]{2,1,0:T(8,128)S(1)} %get-tuple-element.107), channel_id=1, source_target_pairs={{0,8},{8,0},{16,24},{24,16},{32,40},{40,32},{48,56},{56,48},{64,72... | collective-permute-start | bytes 172040 | tf_op jit(solution)/shard_map/ppermute | solution.py:638
  26.5 4.4 %collective-permute-start.5 = (f32[14,8,128]{2,1,0:T(8,128)S(1)}, f32[14,8,128]{2,1,0:T(8,128)S(1)}, u32[]{:S(2)}, u32[]{:S(2)}) collective-permute-start(f32[14,8,128]{2,1,0:T(8,128)S(1)} %get-tuple-element.108), channel_id=1, source_target_pairs={{8,16},{16,8},{24,32},{32,24},{40,48},{48,40},{56,64},{64,56},{72,... | collective-permute-start | bytes 172040 | tf_op jit(solution)/shard_map/ppermute | solution.py:638
  30.9 3.8 %collective-permute-start.6 = (f32[14,8,128]{2,1,0:T(8,128)S(1)}, f32[14,8,128]{2,1,0:T(8,128)S(1)}, u32[]{:S(2)}, u32[]{:S(2)}) collective-permute-start(f32[14,8,128]{2,1,0:T(8,128)S(1)} %get-tuple-element.109), channel_id=1, source_target_pairs={{1,2},{2,1},{3,4},{4,3},{5,6},{6,5},{9,10},{10,9},{11,12},{12,11},... | collective-permute-start | bytes 172040 | tf_op jit(solution)/shard_map/ppermute | solution.py:638
  34.7 0.3 collective-permute-start.7
  35.0 2.2 %second_rest.1 = (f32[9,24,128]{2,1,0:T(8,128)S(1)}, f32[9,24,128]{2,1,0:T(8,128)S(1)}, bf16[288,512]{1,0:T(8,128)(2,1)S(1)}) custom-call(f32[9,9,3,256]{3,2,1,0:T(4,128)S(1)} %get-tuple-element.60.refs_0_, f32[9,9,4,256]{3,2,1,0:T(4,128)S(1)} %get-tuple-element.61.refs_1_, f32[9,9,4,256]{3,2,1,0:T(4,128)S(1)} %get-tuple-element.62.refs_2_, ...), custom_call_target="tpu_custom_call" | custom-call | flops 1000000000 | bytes 1048576 | tf_op jit(solution)/shard_map/second_rest/pallas_call | solution.py:564
  37.2 0.0 collective-permute-done.4.refs_27_
  37.2 0.0 collective-permute-done.5.refs_28_
  37.3 0.0 collective-permute-done.6.refs_29_
  37.3 0.0 collective-permute-done.7.refs_30_
  37.3 6.0 %last.1 = f32[9,20,256]{2,1,0:T(8,128)} custom-call(f32[9,9,3,256]{3,2,1,0:T(4,128)S(1)} %get-tuple-element.60.refs_0_, f32[9,9,4,256]{3,2,1,0:T(4,128)S(1)} %get-tuple-element.61.refs_1_, f32[9,9,4,256]{3,2,1,0:T(4,128)S(1)} %get-tuple-element.62.refs_2_, bf16[80,80]{1,0:T(8,128)(2,1)S(1)} %get-tuple-element.63.refs_3_, ...), custom_call_target="tpu_custom_call" | custom-call | bytes 1048576 | tf_op jit(solution)/shard_map/last/pallas_call | solution.py:564
Async XLA Ops:
  5.3 11.7 %collective-permute-start = (f32[24,8,128]{2,1,0:T(8,128)S(1)}, f32[24,8,128]{2,1,0:T(8,128)S(1)}, u32[]{:S(2)}, u32[]{:S(2)}) collective-permute-start(f32[24,8,128]{2,1,0:T(8,128)S(1)} %get-tuple-element.93), channel_id=1, source_target_pairs={{0,8},{8,0},{16,24},{24,16},{32,40},{40,32},{48,56},{56,48},{64,72... | collective-permute-start | bytes 294920 | tf_op jit(solution)/shard_map/ppermute | solution.py:638
  6.7 10.3 %collective-permute-start.1 = (f32[24,8,128]{2,1,0:T(8,128)S(1)}, f32[24,8,128]{2,1,0:T(8,128)S(1)}, u32[]{:S(2)}, u32[]{:S(2)}) collective-permute-start(f32[24,8,128]{2,1,0:T(8,128)S(1)} %get-tuple-element.94), channel_id=1, source_target_pairs={{8,16},{16,8},{24,32},{32,24},{40,48},{48,40},{56,64},{64,56},{72,... | collective-permute-start | bytes 294920 | tf_op jit(solution)/shard_map/ppermute | solution.py:638
  10.0 7.0 %collective-permute-start.2 = (f32[24,8,128]{2,1,0:T(8,128)S(1)}, f32[24,8,128]{2,1,0:T(8,128)S(1)}, u32[]{:S(2)}, u32[]{:S(2)}) collective-permute-start(f32[24,8,128]{2,1,0:T(8,128)S(1)} %get-tuple-element.95), channel_id=1, source_target_pairs={{1,2},{2,1},{3,4},{4,3},{5,6},{6,5},{9,10},{10,9},{11,12},{12,11},... | collective-permute-start | bytes 294920 | tf_op jit(solution)/shard_map/ppermute | solution.py:638
  14.3 2.7 %collective-permute-start.3 = (f32[24,8,128]{2,1,0:T(8,128)S(1)}, f32[24,8,128]{2,1,0:T(8,128)S(1)}, u32[]{:S(2)}, u32[]{:S(2)}) collective-permute-start(f32[24,8,128]{2,1,0:T(8,128)S(1)} %get-tuple-element.96), channel_id=1, source_target_pairs={{0,1},{1,0},{2,3},{3,2},{4,5},{5,4},{6,7},{7,6},{8,9},{9,8},{10,11... | collective-permute-start | bytes 294920 | tf_op jit(solution)/shard_map/ppermute | solution.py:638
  25.5 11.7 %collective-permute-start.4 = (f32[14,8,128]{2,1,0:T(8,128)S(1)}, f32[14,8,128]{2,1,0:T(8,128)S(1)}, u32[]{:S(2)}, u32[]{:S(2)}) collective-permute-start(f32[14,8,128]{2,1,0:T(8,128)S(1)} %get-tuple-element.107), channel_id=1, source_target_pairs={{0,8},{8,0},{16,24},{24,16},{32,40},{40,32},{48,56},{56,48},{64,72... | collective-permute-start | bytes 172040 | tf_op jit(solution)/shard_map/ppermute | solution.py:638
  26.5 10.8 %collective-permute-start.5 = (f32[14,8,128]{2,1,0:T(8,128)S(1)}, f32[14,8,128]{2,1,0:T(8,128)S(1)}, u32[]{:S(2)}, u32[]{:S(2)}) collective-permute-start(f32[14,8,128]{2,1,0:T(8,128)S(1)} %get-tuple-element.108), channel_id=1, source_target_pairs={{8,16},{16,8},{24,32},{32,24},{40,48},{48,40},{56,64},{64,56},{72,... | collective-permute-start | bytes 172040 | tf_op jit(solution)/shard_map/ppermute | solution.py:638
  30.9 6.4 %collective-permute-start.6 = (f32[14,8,128]{2,1,0:T(8,128)S(1)}, f32[14,8,128]{2,1,0:T(8,128)S(1)}, u32[]{:S(2)}, u32[]{:S(2)}) collective-permute-start(f32[14,8,128]{2,1,0:T(8,128)S(1)} %get-tuple-element.109), channel_id=1, source_target_pairs={{1,2},{2,1},{3,4},{4,3},{5,6},{6,5},{9,10},{10,9},{11,12},{12,11},... | collective-permute-start | bytes 172040 | tf_op jit(solution)/shard_map/ppermute | solution.py:638
  34.7 2.6 %collective-permute-start.7 = (f32[14,8,128]{2,1,0:T(8,128)S(1)}, f32[14,8,128]{2,1,0:T(8,128)S(1)}, u32[]{:S(2)}, u32[]{:S(2)}) collective-permute-start(f32[14,8,128]{2,1,0:T(8,128)S(1)} %get-tuple-element.110), channel_id=1, source_target_pairs={{0,1},{1,0},{2,3},{3,2},{4,5},{5,4},{6,7},{7,6},{8,9},{9,8},{10,11... | collective-permute-start | bytes 172040 | tf_op jit(solution)/shard_map/ppermute | solution.py:638

commit v3 on v2

--- a/solution.py
+++ b/solution.py
@@ -14,6 +14,7 @@
 B = 24
 FB = 16
 LANES = 128
+TABLE = 96
 KZ = 160
 STATIC = 42
 F32 = jnp.float32
@@ -287,36 +288,53 @@
             s.pick("moved", lg)[q] = half[0 : 3 * B]
             for j in range(4):
                 s.pick("face", lg)[j, q] = half[3 * B + FB * j : 3 * B + FB * (j + 1)]
+    for lg in range(2):
+        face = s.pick("face", lg)
         for j in range(4):
-            high, low = halves(got[3 * B + FB * j : 3 * B + FB * (j + 1)])
-            s.table[q * FB : (q + 1) * FB, j * 256 : (j + 1) * 256] = high
-            s.table[(Q + q) * FB : (Q + q + 1) * FB, j * 256 : (j + 1) * 256] = low
-
-
-def change_of(base, out, r, s, groups):
-    rows = Q * FB
+            blocks = [face[j, q, 0:8] for q in range(Q)]
+            blocks += [by_face([face[j, min(q + n, Q - 1), 8:16] for n in range(4)]) for q in range(0, Q, 4)]
+            cols = group(2 * j + lg)
+            for n in range(0, 12, 2):
+                high, low = halves(jnp.concatenate(blocks[n : n + 2], axis=0))
+                s.table[8 * n : 8 * n + 16, cols] = high
+                s.table[TABLE + 8 * n : TABLE + 8 * n + 16, cols] = low
+
+
+def change_of(base, out, r, s, groups, finish=None):
+    def keep(p, lg, value):
+        out[lg][p] = value
+
+    finish = finish or keep
     for lg in groups:
         for pair in range(2):
             cols = pl.ds(2 * pair * LANES, 2 * LANES)
             got = mm(s.table[...], s.pick("hot", lg)[:, cols])
-            total = got[0:rows] + got[rows : 2 * rows]
+            total = got[0:TABLE] + got[TABLE : 2 * TABLE]
             for half in range(2):
                 s.across[2 * pair + half] = total[:, half * LANES : (half + 1) * LANES]
         face, across = s.pick("face", lg), s.across
+
+        def last_own(q):
+            return by_face([face[k, q, 8:16] for k in range(4)])
+
+        def last_across(q):
+            at = Q * 8 + q // 4 * 8
+            found = [across[k, at : at + 8] for k in range(4)]
+            if q < 8:
+                found = [pltpu.roll(f, (k - q % 4) % 8, 0) if k != q % 4 else f for k, f in enumerate(found)]
+            return by_face(found)
+
         sources = (
-            (r.fluxl, s.pick("fpl", lg), lambda i, q, rows: face[i, q, rows]),
-            (r.fluxn, s.pick("fpn", lg), lambda i, q, rows: across[i, q * FB + rows.start : q * FB + rows.stop]),
+            (r.fluxl, s.pick("fpl", lg), lambda i, q: face[i, q, 0:8], last_own),
+            (r.fluxn, s.pick("fpn", lg), lambda i, q: across[i, q * 8 : (q + 1) * 8], last_across),
         )
         got = []
-        for flux_ref, rows_ref, field in sources:
+        for flux_ref, rows_ref, main, last in sources:
             sums = []
             for i in range(5):
                 acc = [None] * Q
                 for q in range(Q):
-                    if i < 4:
-                        value = field(i, q, slice(0, 8))
-                    else:
-                        value = by_face([field(k, q, slice(8, 16)) for k in range(4)])
+                    value = main(i, q) if i < 4 else last(q)
                     for p in range(Q):
                         scale = flux_ref[p, q, i : i + 1, group(lg)] if i < 4 else rows_ref[p * Q + q]
                         term = scale * value
@@ -339,7 +357,7 @@
 
     def store(p, total):
         for n, lg in enumerate(groups):
-            out[lg][p] = out[lg][p] - total[:, n * LANES : (n + 1) * LANES]
+            finish(p, lg, out[lg][p] - total[:, n * LANES : (n + 1) * LANES])
 
     lift(r.wl, s.zh, s.zl, len(groups) * LANES, store)
 
@@ -450,7 +468,7 @@
     predict(o.part1, [own_star(r.star, 1)], r.wt, s.term1, s.pmoved1, [(o.ahead, FIRST)])
 
 
-def odd_half(s, r, fine, ghost_ref, outs):
+def odd_half(s, r, fine, ghost_ref, outs, finish=None):
     def keep_table(n, value):
         s.gfield[n // 3, 8 * (n % 3) : 8 * (n % 3) + 8, :] = value
 
@@ -488,7 +506,7 @@
         s.dofs[p, :, 0:LANES] = s.dofs[p, :, 0:LANES] - total
 
     lift(r.wl, s.rzh, s.rzl, LANES, second_store)
-    change_of([s.dofs.at[:, :, 0:LANES], r.part1], outs, r, s, [0, 1])
+    change_of([s.dofs.at[:, :, 0:LANES], r.part1], outs, r, s, [0, 1], finish)
 
 
 FIELD = ((Q, B, LANES), F32)
@@ -499,10 +517,10 @@
 KEPT = dict(
     moved1=((Q, 3 * B, LANES), F32),
     face1=((4, Q, FB, LANES), F32),
-    table=((2 * Q * FB, 1024), BF16),
+    table=((2 * TABLE, 1024), BF16),
 )
 CHANGE = dict(
-    across=((4, Q * FB, LANES), F32),
+    across=((4, TABLE, LANES), F32),
     zh=((KZ, Q * 256), BF16),
     zl=((KZ, Q * 256), BF16),
 )
@@ -538,7 +556,7 @@
     return {key: ((blocks // 4, 8, LANES), F32) for key in SENT}
 
 
-def call(kernel, name, ins, outs, scratch, inputs, columns, hbm=False, flops=0):
+def call(kernel, name, ins, outs, scratch, inputs, columns, hbm=False, flops=0, outside=False):
     def body(*refs):
         n, m = len(ins), len(outs)
         r = Bag(zip(ins, refs[:n]))
@@ -557,7 +575,7 @@
             r.even = place_of(r.nbr, columns)
             kernel(r, o, s)
 
-    shapes = [pltpu.VMEM(*scratch[key]) for key in scratch]
+    shapes = [pltpu.VMEM(*value) if isinstance(value, tuple) else value for value in scratch.values()]
     if hbm:
         shapes.append(pltpu.SemaphoreType.DMA((len(ins),)))
     space = pltpu.HBM if hbm else pltpu.VMEM
@@ -565,7 +583,7 @@
         body,
         out_shape=[jax.ShapeDtypeStruct(*outs[key]) for key in outs],
         in_specs=[pl.BlockSpec(memory_space=space)] * len(ins),
-        out_specs=[pl.BlockSpec(memory_space=pltpu.VMEM)] * len(outs),
+        out_specs=[pl.BlockSpec(memory_space=pltpu.HBM if outside else pltpu.VMEM)] * len(outs),
         scratch_shapes=shapes,
         compiler_params=pltpu.CompilerParams(vmem_limit_bytes=24 << 20),
         cost_estimate=pl.CostEstimate(flops=flops, bytes_accessed=1 << 20, transcendentals=0),
@@ -622,10 +640,17 @@
 
 
 def last_kernel(r, o, s):
+    copies = [pltpu.make_async_copy(s.result.at[p], o.out.at[p], s.sems.at[p]) for p in range(Q)]
+
+    def finish(p, lg, value):
+        s.result[p, :, group(lg)] = value[0:20]
+        if lg == 1:
+            copies[p].start()
+
     s = r | s
-    odd_half(s, r, fine_of(r.cluster), r.ghost, [s.next.at[:, :, group(lg)] for lg in range(2)])
-    for p in range(Q):
-        o.out[p] = s.next[p, 0:20, :]
+    odd_half(s, r, fine_of(r.cluster), r.ghost, [s.next.at[:, :, group(lg)] for lg in range(2)], finish)
+    for copy in copies:
+        copy.wait()
 
 
 def trade(got):
@@ -683,7 +708,8 @@
         flops=10**9,
     )
     got = call(
-        last_kernel, "last", odd + ["ghost", *GHOST_MASKS], {"out": ((Q, 20, 256), F32)}, {**both, **KEPT}, inputs, columns,
+        last_kernel, "last", odd + ["ghost", *GHOST_MASKS], {"out": ((Q, 20, 256), F32)}, {**both, **KEPT, "result": ((Q, 20, 256), F32), "sems": pltpu.SemaphoreType.DMA((Q,))},
+        inputs, columns, outside=True,
     )
     return got["out"]
 

time: 43.7 us -> 43.4 us (level)
  no operation moved by 1% of the time
where the time goes in v3:
time: 43.4 us; the launch traced here: 43 us
  Pallas kernels  24 us (55%)
  starting transfers between devices  18.7 us (43%)
    pallas_call x5, Pallas kernels, call(): pl.pallas_call(body, out_shape=[jax.ShapeDtypeStruct(*outs[key]) for key...  24 us
    ppermute x8, starting transfers between devices, trade(): out[GOT[m]] = lax.ppermute(got[SENT[m]], axis, pairs)  18.7 us
  transfers between devices with their start and end apart: 8, of which 0 were waited for; matrix products, arithmetic and copies ran while one was open for 0% of the time, Pallas kernels for 11%

profile of v3, /device:TPU:129, one launch (start us, length us, event | category | flops | bytes accessed | tf_op | source)
XLA Modules:
  0.0 43.0 jit_solution(4827009407054781058)
XLA Ops:
  0.0 5.2 %first.1 = (f32[9,9,3,256]{3,2,1,0:T(4,128)S(1)}, f32[9,9,4,256]{3,2,1,0:T(4,128)S(1)}, f32[9,9,4,256]{3,2,1,0:T(4,128)S(1)}, s32[4,256]{1,0:T(4,128)S(1)}, s32[...) custom-call(f32[9,20,256]{2,1,0:T(8,128)} %refs_0_.1, ...), custom_call_target="tpu_custom_call" | custom-call | bytes 1048576 | tf_op jit(solution)/shard_map/first/pallas_call | solution.py:582
  5.2 1.4 %collective-permute-start = (f32[24,8,128]{2,1,0:T(8,128)S(1)}, f32[24,8,128]{2,1,0:T(8,128)S(1)}, u32[]{:S(2)}, u32[]{:S(2)}) collective-permute-start(f32[24,8,128]{2,1,0:T(8,128)S(1)} %get-tuple-element.93), channel_id=1, source_target_pairs={{0,8},{8,0},{16,24},{24,16},{32,40},{40,32},{48,56},{56,48},{64,72... | collective-permute-start | bytes 294920 | tf_op jit(solution)/shard_map/ppermute | solution.py:663
  6.6 3.3 %collective-permute-start.1 = (f32[24,8,128]{2,1,0:T(8,128)S(1)}, f32[24,8,128]{2,1,0:T(8,128)S(1)}, u32[]{:S(2)}, u32[]{:S(2)}) collective-permute-start(f32[24,8,128]{2,1,0:T(8,128)S(1)} %get-tuple-element.94), channel_id=1, source_target_pairs={{8,16},{16,8},{24,32},{32,24},{40,48},{48,40},{56,64},{64,56},{72,... | collective-permute-start | bytes 294920 | tf_op jit(solution)/shard_map/ppermute | solution.py:663
  10.0 4.2 %collective-permute-start.2 = (f32[24,8,128]{2,1,0:T(8,128)S(1)}, f32[24,8,128]{2,1,0:T(8,128)S(1)}, u32[]{:S(2)}, u32[]{:S(2)}) collective-permute-start(f32[24,8,128]{2,1,0:T(8,128)S(1)} %get-tuple-element.95), channel_id=1, source_target_pairs={{1,2},{2,1},{3,4},{4,3},{5,6},{6,5},{9,10},{10,9},{11,12},{12,11},... | collective-permute-start | bytes 294920 | tf_op jit(solution)/shard_map/ppermute | solution.py:663
  14.2 0.3 collective-permute-start.3
  14.5 2.4 %first_rest.1 = (f32[9,24,128]{2,1,0:T(8,128)S(1)}, f32[9,24,128]{2,1,0:T(8,128)S(1)}, bf16[288,512]{1,0:T(8,128)(2,1)S(1)}, bf16[1024,512]{1,0:T(8,128)(2,1)S(1...) custom-call(f32[9,9,3,256]{3,2,1,0:T(4,128)S(1)} %get-tuple-element., ...), custom_call_target="tpu_custom_call" | custom-call | flops 1000000000 | bytes 1048576 | tf_op jit(solution)/shard_map/first_rest/pallas_call | solution.py:582
  16.9 0.0 collective-permute-done.refs_27_
  16.9 0.0 collective-permute-done.1.refs_28_
  16.9 0.0 collective-permute-done.2.refs_29_
  17.0 0.0 collective-permute-done.3.refs_30_
  17.0 8.4 %middle.1 = (f32[42,8,128]{2,1,0:T(8,128)S(1)}, bf16[512,128]{1,0:T(8,128)(2,1)S(1)}, bf16[6,16,128]{2,1,0:T(8,128)(2,1)S(1)}, f32[3,8,128]{2,1,0:T(8,128)S(1)},...) custom-call(f32[9,9,3,256]{3,2,1,0:T(4,128)S(1)} %get-tuple-element., ...), custom_call_target="tpu_custom_call" | custom-call | bytes 1048576 | tf_op jit(solution)/shard_map/middle/pallas_call | solution.py:582
  25.3 0.9 %collective-permute-start.4 = (f32[14,8,128]{2,1,0:T(8,128)S(1)}, f32[14,8,128]{2,1,0:T(8,128)S(1)}, u32[]{:S(2)}, u32[]{:S(2)}) collective-permute-start(f32[14,8,128]{2,1,0:T(8,128)S(1)} %get-tuple-element.107), channel_id=1, source_target_pairs={{0,8},{8,0},{16,24},{24,16},{32,40},{40,32},{48,56},{56,48},{64,72... | collective-permute-start | bytes 172040 | tf_op jit(solution)/shard_map/ppermute | solution.py:663
  26.3 4.4 %collective-permute-start.5 = (f32[14,8,128]{2,1,0:T(8,128)S(1)}, f32[14,8,128]{2,1,0:T(8,128)S(1)}, u32[]{:S(2)}, u32[]{:S(2)}) collective-permute-start(f32[14,8,128]{2,1,0:T(8,128)S(1)} %get-tuple-element.108), channel_id=1, source_target_pairs={{8,16},{16,8},{24,32},{32,24},{40,48},{48,40},{56,64},{64,56},{72,... | collective-permute-start | bytes 172040 | tf_op jit(solution)/shard_map/ppermute | solution.py:663
  30.7 3.8 %collective-permute-start.6 = (f32[14,8,128]{2,1,0:T(8,128)S(1)}, f32[14,8,128]{2,1,0:T(8,128)S(1)}, u32[]{:S(2)}, u32[]{:S(2)}) collective-permute-start(f32[14,8,128]{2,1,0:T(8,128)S(1)} %get-tuple-element.109), channel_id=1, source_target_pairs={{1,2},{2,1},{3,4},{4,3},{5,6},{6,5},{9,10},{10,9},{11,12},{12,11},... | collective-permute-start | bytes 172040 | tf_op jit(solution)/shard_map/ppermute | solution.py:663
  34.5 0.3 collective-permute-start.7
  34.8 2.1 %second_rest.1 = (f32[9,24,128]{2,1,0:T(8,128)S(1)}, f32[9,24,128]{2,1,0:T(8,128)S(1)}, bf16[288,512]{1,0:T(8,128)(2,1)S(1)}) custom-call(f32[9,9,3,256]{3,2,1,0:T(4,128)S(1)} %get-tuple-element.60.refs_0_, f32[9,9,4,256]{3,2,1,0:T(4,128)S(1)} %get-tuple-element.61.refs_1_, f32[9,9,4,256]{3,2,1,0:T(4,128)S(1)} %get-tuple-element.62.refs_2_, ...), custom_call_target="tpu_custom_call" | custom-call | flops 1000000000 | bytes 1048576 | tf_op jit(solution)/shard_map/second_rest/pallas_call | solution.py:582
  36.9 0.0 collective-permute-done.4.refs_27_
  36.9 0.0 collective-permute-done.5.refs_28_
  36.9 0.0 collective-permute-done.6.refs_29_
  36.9 0.0 collective-permute-done.7.refs_30_
  36.9 5.8 %last.1 = f32[9,20,256]{2,1,0:T(8,128)} custom-call(f32[9,9,3,256]{3,2,1,0:T(4,128)S(1)} %get-tuple-element.60.refs_0_, f32[9,9,4,256]{3,2,1,0:T(4,128)S(1)} %get-tuple-element.61.refs_1_, f32[9,9,4,256]{3,2,1,0:T(4,128)S(1)} %get-tuple-element.62.refs_2_, bf16[80,80]{1,0:T(8,128)(2,1)S(1)} %get-tuple-element.63.refs_3_, ...), custom_call_target="tpu_custom_call" | custom-call | bytes 1048576 | tf_op jit(solution)/shard_map/last/pallas_call | solution.py:582
Async XLA Ops:
  5.2 11.7 %collective-permute-start = (f32[24,8,128]{2,1,0:T(8,128)S(1)}, f32[24,8,128]{2,1,0:T(8,128)S(1)}, u32[]{:S(2)}, u32[]{:S(2)}) collective-permute-start(f32[24,8,128]{2,1,0:T(8,128)S(1)} %get-tuple-element.93), channel_id=1, source_target_pairs={{0,8},{8,0},{16,24},{24,16},{32,40},{40,32},{48,56},{56,48},{64,72... | collective-permute-start | bytes 294920 | tf_op jit(solution)/shard_map/ppermute | solution.py:663
  6.6 10.3 %collective-permute-start.1 = (f32[24,8,128]{2,1,0:T(8,128)S(1)}, f32[24,8,128]{2,1,0:T(8,128)S(1)}, u32[]{:S(2)}, u32[]{:S(2)}) collective-permute-start(f32[24,8,128]{2,1,0:T(8,128)S(1)} %get-tuple-element.94), channel_id=1, source_target_pairs={{8,16},{16,8},{24,32},{32,24},{40,48},{48,40},{56,64},{64,56},{72,... | collective-permute-start | bytes 294920 | tf_op jit(solution)/shard_map/ppermute | solution.py:663
  10.0 7.0 %collective-permute-start.2 = (f32[24,8,128]{2,1,0:T(8,128)S(1)}, f32[24,8,128]{2,1,0:T(8,128)S(1)}, u32[]{:S(2)}, u32[]{:S(2)}) collective-permute-start(f32[24,8,128]{2,1,0:T(8,128)S(1)} %get-tuple-element.95), channel_id=1, source_target_pairs={{1,2},{2,1},{3,4},{4,3},{5,6},{6,5},{9,10},{10,9},{11,12},{12,11},... | collective-permute-start | bytes 294920 | tf_op jit(solution)/shard_map/ppermute | solution.py:663
  14.2 2.7 %collective-permute-start.3 = (f32[24,8,128]{2,1,0:T(8,128)S(1)}, f32[24,8,128]{2,1,0:T(8,128)S(1)}, u32[]{:S(2)}, u32[]{:S(2)}) collective-permute-start(f32[24,8,128]{2,1,0:T(8,128)S(1)} %get-tuple-element.96), channel_id=1, source_target_pairs={{0,1},{1,0},{2,3},{3,2},{4,5},{5,4},{6,7},{7,6},{8,9},{9,8},{10,11... | collective-permute-start | bytes 294920 | tf_op jit(solution)/shard_map/ppermute | solution.py:663
  25.3 11.6 %collective-permute-start.4 = (f32[14,8,128]{2,1,0:T(8,128)S(1)}, f32[14,8,128]{2,1,0:T(8,128)S(1)}, u32[]{:S(2)}, u32[]{:S(2)}) collective-permute-start(f32[14,8,128]{2,1,0:T(8,128)S(1)} %get-tuple-element.107), channel_id=1, source_target_pairs={{0,8},{8,0},{16,24},{24,16},{32,40},{40,32},{48,56},{56,48},{64,72... | collective-permute-start | bytes 172040 | tf_op jit(solution)/shard_map/ppermute | solution.py:663
  26.3 10.6 %collective-permute-start.5 = (f32[14,8,128]{2,1,0:T(8,128)S(1)}, f32[14,8,128]{2,1,0:T(8,128)S(1)}, u32[]{:S(2)}, u32[]{:S(2)}) collective-permute-start(f32[14,8,128]{2,1,0:T(8,128)S(1)} %get-tuple-element.108), channel_id=1, source_target_pairs={{8,16},{16,8},{24,32},{32,24},{40,48},{48,40},{56,64},{64,56},{72,... | collective-permute-start | bytes 172040 | tf_op jit(solution)/shard_map/ppermute | solution.py:663
  30.7 6.3 %collective-permute-start.6 = (f32[14,8,128]{2,1,0:T(8,128)S(1)}, f32[14,8,128]{2,1,0:T(8,128)S(1)}, u32[]{:S(2)}, u32[]{:S(2)}) collective-permute-start(f32[14,8,128]{2,1,0:T(8,128)S(1)} %get-tuple-element.109), channel_id=1, source_target_pairs={{1,2},{2,1},{3,4},{4,3},{5,6},{6,5},{9,10},{10,9},{11,12},{12,11},... | collective-permute-start | bytes 172040 | tf_op jit(solution)/shard_map/ppermute | solution.py:663
  34.5 2.5 %collective-permute-start.7 = (f32[14,8,128]{2,1,0:T(8,128)S(1)}, f32[14,8,128]{2,1,0:T(8,128)S(1)}, u32[]{:S(2)}, u32[]{:S(2)}) collective-permute-start(f32[14,8,128]{2,1,0:T(8,128)S(1)} %get-tuple-element.110), channel_id=1, source_target_pairs={{0,1},{1,0},{2,3},{3,2},{4,5},{5,4},{6,7},{7,6},{8,9},{9,8},{10,11... | collective-permute-start | bytes 172040 | tf_op jit(solution)/shard_map/ppermute | solution.py:663
